TPU v7x, 128 devices: a whole 4x4x4 slice. The times are simulated.
128 devices in a mesh: seq: 32 (over z, y, core), head: 4 (over x).
Axes of the slice: x: 4, y: 4, z: 4, core: 2. Of those that a mesh axis runs over, the one named last changes fastest.
Arguments:
- tokens: bfloat16 [8192, 4096], P('seq', 'head'), may hold values from -48 to 48
- queries: bfloat16 [8192, 4096], P('seq', 'head'), may hold values from -48 to 48
- valid_counts: int32 [32], P('seq'), may hold values from 64 to 256, as said below
- query_host: int32 [1], replicated, may hold values from 0 to 31
- w_query: bfloat16 [4096, 4096], P(None, 'head'), may hold values from -0.09375 to 0.09375
- w_key: bfloat16 [4096, 1024], P(None, 'head'), may hold values from -0.09375 to 0.09375
- w_value: bfloat16 [4096, 1024], P(None, 'head'), may hold values from -0.09375 to 0.09375
- w_out: bfloat16 [4096, 4096], P('head'), may hold values from -0.09375 to 0.09375
Outputs:
- block_out: bfloat16 [8192, 4096], P('seq', 'head')
- query_out: bfloat16 [256, 4096], P(None, 'head')
Inputs may be any that keep to these rules, and one draw needn't show every extreme that they name: `valid_counts`: some block has all 256 tokens valid.
All inputs are finite; a program needn't handle non-finite values.
Results may differ from a plain program's by a relative error of at most 0.014.
The roundings to bfloat16 on the way count: a program that leaves them out, or rounds other values in their place, can miss the bound.
Values may be sent and summed in bfloat16 or wider, within the bound.
No kernel may reach another device: no remote copies, remote signals or barrier semaphores. Data moves between devices by JAX's collectives and lax.ppermute only.
A program may use at most 192 MiB of HBM per device.

v0:
```python
import jax
import jax.numpy as jnp
from jax import lax
from jax.experimental import pallas as pl
from jax.experimental.pallas import tpu as pltpu
from jax.sharding import PartitionSpec as P

HD = 128
LOG2_SCALE = HD ** (-0.5) * 1.4426950408889634
NEG = -1e30
PAIRS = 16
PLANE = [[2 * g + c for g in range(PAIRS)] for c in range(2)]
SWAP = [(i, i ^ 1) for i in range(2 * PAIRS)]
MIB = 1 << 20
VMEM = pl.BlockSpec(memory_space=pltpu.VMEM)
SMEM = pl.BlockSpec(memory_space=pltpu.SMEM)
ANY = pl.BlockSpec(memory_space=pl.ANY)
HBM = pl.BlockSpec(memory_space=pltpu.HBM)


def params(mib=52):
    return pltpu.CompilerParams(vmem_limit_bytes=mib * MIB)


def cost(flops, moved):
    return pl.CostEstimate(flops=flops, bytes_accessed=moved, transcendentals=0)


def plane_swap(blocks):
    return lax.all_to_all(blocks, "seq", 0, 0, axis_index_groups=PLANE, tiled=True)


def core_swap(block):
    return lax.ppermute(block, "seq", SWAP)


def head_shift(block, step):
    return lax.ppermute(block, "head", [(i, (i + step) % 4) for i in range(4)])


def exact_dot(a, b):
    return lax.dot_general(a, b, (((1,), (0,)), ((), ())), preferred_element_type=jnp.float32)


def score_dot(a, b):
    return lax.dot_general(a, b, (((1,), (1,)), ((), ())), preferred_element_type=jnp.float32)


def choose_kernel(counts, queries, tokens, out, held, sem):
    @pl.when(lax.axis_index("seq") == 0)
    def _():
        copy = pltpu.make_async_copy(tokens, held, sem)
        copy.start()
        copy.wait()
        row = lax.broadcasted_iota(jnp.int32, out.shape, 0)
        rows = held[...].astype(jnp.float32)
        out[...] = jnp.where(row < counts[0], rows, jnp.nan).astype(out.dtype)

    @pl.when(lax.axis_index("seq") != 0)
    def _():
        copy = pltpu.make_async_copy(queries, out, sem)
        copy.start()
        copy.wait()


def choose(counts, queries, tokens):
    return pl.pallas_call(
        choose_kernel,
        in_specs=[SMEM, ANY, ANY],
        out_specs=VMEM,
        out_shape=jax.ShapeDtypeStruct(tokens.shape, tokens.dtype),
        scratch_shapes=[pltpu.VMEM(tokens.shape, tokens.dtype), pltpu.SemaphoreType.DMA],
        compiler_params=params(4),
        cost_estimate=cost(1000, 2 * MIB),
    )(counts, queries, tokens)


def start_all(copies):
    for copy in copies:
        copy.start()
    return copies


def rows_of(step, size):
    return pl.ds(pl.multiple_of(((lax.axis_index("head") - step + 4) % 4) * size, size), size)


def few_kernel(fews, wq, wk, wv, pack_out, kv_out, held_q, held_kv, sems):
    size = fews.shape[2]
    nk = wk.shape[1]
    copies = []
    for step in range(4):
        rows = pl.ds(step * size, size)
        copies.append(
            start_all(
                [
                    pltpu.make_async_copy(wq.at[rows], held_q.at[step], sems.at[step, 0]),
                    pltpu.make_async_copy(wk.at[rows], held_kv.at[step, 0], sems.at[step, 1]),
                    pltpu.make_async_copy(wv.at[rows], held_kv.at[step, 1], sems.at[step, 2]),
                ]
            )
        )
    q = k = v = 0.0
    for step in range(4):
        for copy in copies[step]:
            copy.wait()
        few = fews[step]
        q += exact_dot(few, held_q[step])
        k += exact_dot(few, held_kv[step, 0])
        v += exact_dot(few, held_kv[step, 1])
    slab = fews.shape[1] // 2
    pack = jnp.concatenate([q[:slab], k[slab:], v[slab:]], axis=1)
    pack_out[...] = jnp.broadcast_to(pack[None], pack_out.shape).astype(pack_out.dtype)
    own = jnp.concatenate([k[:slab], v[:slab]], axis=1)
    kv_out[...] = jnp.concatenate([own, jnp.zeros_like(own)], axis=0).astype(kv_out.dtype)


def project_few(fews, w_query, w_key, w_value):
    depth = w_query.shape[0]
    few, size = fews.shape[1:]
    nq, nk = w_query.shape[1], w_key.shape[1]
    dtype = w_query.dtype
    return pl.pallas_call(
        few_kernel,
        in_specs=[VMEM] + [HBM] * 3,
        out_specs=[VMEM] * 2,
        out_shape=[
            jax.ShapeDtypeStruct((PAIRS, few // 2, nq + 2 * nk), dtype),
            jax.ShapeDtypeStruct((few, 2 * nk), dtype),
        ],
        scratch_shapes=[
            pltpu.VMEM((4, size, nq), dtype),
            pltpu.VMEM((4, 2, size, nk), dtype),
            pltpu.SemaphoreType.DMA((4, 3)),
        ],
        compiler_params=params(),
        cost_estimate=cost(2 * 128 * depth * (nq + 2 * nk), depth * (nq + 2 * nk) * 2),
    )(fews, w_query, w_key, w_value)


def chunk_copies(chunk, held, sems, at):
    half = chunk[0].shape[0]
    return [
        pltpu.make_async_copy(part, held.at[pl.ds(i * half, half)], sems.at[at + i])
        for i, part in enumerate(chunk)
    ]


def keys_kernel(*refs):
    (c0, c1, c2a, c2b, c3), (wk, wv, few, out, held, held_kv, acc, sems) = refs[:5], refs[5:]
    count, size = held.shape[1:]
    chunks = (c0,), (c1,), (c2a, c2b), (c3,)
    nk = wk.shape[1]
    copies = []
    for step in range(4):
        rows = rows_of(step, size)
        copies.append(
            start_all(
                [
                    pltpu.make_async_copy(wk.at[rows], held_kv.at[step, 0], sems.at[step, 0]),
                    pltpu.make_async_copy(wv.at[rows], held_kv.at[step, 1], sems.at[step, 1]),
                ]
                + chunk_copies(chunks[step], held.at[step], sems.at[step], 2)
            )
        )
    for step in range(4):
        for copy in copies[step]:
            copy.wait()
        for part in range(2):
            here = pl.ds(part * nk, nk)
            term = exact_dot(held[step], held_kv[step, part])
            if step == 0:
                acc[:, here] = term
            elif step < 3:
                acc[:, here] += term
            else:
                out[:count, here] = (acc[:, here] + term).astype(out.dtype)
    out[count:, :] = few[...]


def project_keys(chunks, w_key, w_value, few):
    rows, size = chunks[0].shape
    nk = w_key.shape[1]
    shape = (rows + few.shape[0], 2 * nk)
    dtype = w_key.dtype
    return pl.pallas_call(
        keys_kernel,
        in_specs=[ANY] * 5 + [HBM] * 2 + [VMEM],
        out_specs=VMEM,
        out_shape=jax.ShapeDtypeStruct(shape, dtype),
        scratch_shapes=[
            pltpu.VMEM((4, rows, size), dtype),
            pltpu.VMEM((4, 2, size, nk), dtype),
            pltpu.VMEM((rows, 2 * nk), jnp.float32),
            pltpu.SemaphoreType.DMA((4, 4)),
        ],
        compiler_params=params(),
        cost_estimate=cost(2 * rows * 4 * size * 2 * nk, 6 * MIB),
    )(*chunks, w_key, w_value, few)


def queries_kernel(*refs):
    (c0, c1, c2a, c2b, c3), (wq, out, held, held_q, acc, sems) = refs[:5], refs[5:]
    count, size = held.shape[1:]
    chunks = (c0,), (c1,), (c2a, c2b), (c3,)
    copies = []
    for step in range(4):
        rows = rows_of(step, size)
        copies.append(
            start_all(
                [
                    pltpu.make_async_copy(wq.at[rows], held_q.at[step], sems.at[step, 0]),
                ]
                + chunk_copies(chunks[step], held.at[step], sems.at[step], 1)
            )
        )
    for step in range(4):
        for copy in copies[step]:
            copy.wait()
        term = exact_dot(held[step], held_q[step])
        if step == 0:
            acc[...] = term
        elif step < 3:
            acc[...] += term
        else:
            out[...] = (acc[...] + term).astype(out.dtype)


def project_queries(chunks, w_query):
    rows, size = chunks[0].shape
    wide = w_query.shape[1]
    dtype = w_query.dtype
    return pl.pallas_call(
        queries_kernel,
        in_specs=[ANY] * 5 + [HBM],
        out_specs=VMEM,
        out_shape=jax.ShapeDtypeStruct((rows, wide), dtype),
        scratch_shapes=[
            pltpu.VMEM((4, rows, size), dtype),
            pltpu.VMEM((4, size, wide), dtype),
            pltpu.VMEM((rows, wide), jnp.float32),
            pltpu.SemaphoreType.DMA((4, 3)),
        ],
        compiler_params=params(),
        cost_estimate=cost(2 * rows * 4 * size * wide, 10 * MIB),
    )(*chunks, w_query)


def split(x):
    high = x.astype(jnp.bfloat16).astype(jnp.float32)
    middle = (x - high).astype(jnp.bfloat16).astype(jnp.float32)
    return [high, middle, x - high - middle]


def query_kernel(counts, sibling, q_ref, mine, other, out):
    seq = lax.axis_index("seq")
    core, pair, count_mine, count_other = seq % 2, seq // 2, counts[0], sibling[0]
    half = q_ref.shape[0]
    blk = 2 * half
    nk = mine.shape[1] // 2
    few = mine.shape[0] - blk
    slab = few // 2
    groups = nk // HD
    heads = (q_ref.shape[1] - 2 * nk) // HD
    local_row = lax.broadcasted_iota(jnp.int32, (HD, 2 * half), 1) % half
    row = local_row + slab * (local_row // slab + core)
    key = lax.broadcasted_iota(jnp.int32, (HD, 2 * half), 0)
    first = (2 * pair + core) * slab
    first_other = (2 * pair + 1 - core) * slab
    own_a = (key < slab) & (first + key <= row)
    own_b = (key >= few) & (key < few + slab) & (first_other + key - few <= row)
    block_key = lax.broadcasted_iota(jnp.int32, (blk, 2 * half), 0)
    seen = jnp.concatenate([block_key < count_mine, block_key < count_other, own_a | own_b], axis=0)
    fill = jnp.zeros((HD - 2 * few, HD), mine.dtype)
    tops, totals = [], []
    for g in range(groups):
        keys, values = (
            jnp.concatenate(
                [mine[:blk, c], other[:blk, c], mine[blk:, c], other[blk:, c], fill], axis=0
            )
            for c in (pl.ds(g * HD, HD), pl.ds(nk + g * HD, HD))
        )
        values = values.T
        for h in range(g * (heads // groups), (g + 1) * (heads // groups), 2):
            q = jnp.concatenate([q_ref[:, pl.ds((h + i) * HD, HD)] for i in range(2)], axis=0)
            s = jnp.where(seen, score_dot(keys, q), NEG)
            top = jnp.max(s, axis=0, keepdims=True)
            p = jnp.exp2((s - top) * LOG2_SCALE).astype(mine.dtype)
            total = jnp.sum(p.astype(jnp.float32), axis=0, keepdims=True)
            o = exact_dot(values, p).T.astype(out.dtype)
            for i in range(2):
                out[:, pl.ds((h + i) * HD, HD)] = o[i * half : (i + 1) * half]
                tops.append(top[:, i * half : (i + 1) * half])
                totals.append(total[:, i * half : (i + 1) * half])
    stats = [part for x in (tops, totals) for part in split(jnp.concatenate(x, axis=0))]
    pad = jnp.zeros((HD - 6 * heads, half), jnp.float32)
    out[:, pl.ds(heads * HD, HD)] = jnp.concatenate(stats + [pad], axis=0).T.astype(out.dtype)


def query_attention(counts, sibling, mine_rows, kv, kv_other):
    rows, wide = mine_rows.shape
    nq = wide - kv.shape[1]
    return pl.pallas_call(
        query_kernel,
        in_specs=[SMEM] * 2 + [VMEM] * 3,
        out_specs=VMEM,
        out_shape=jax.ShapeDtypeStruct((rows, nq + HD), kv.dtype),
        compiler_params=params(24),
        cost_estimate=cost(4 * rows * 640 * nq, 4 * MIB),
    )(counts, sibling, mine_rows, kv, kv_other)


ORDER = (2, 1, 3, 0)


def columns_of(step, size):
    return pl.ds(pl.multiple_of(((lax.axis_index("head") + step) % 4) * size, size), size)


def context_kernel(
    counts, q_ref, kv, a_mine, a_other, w_ref, out0, out1, out2, own, ctx, held, sems
):
    seq, count = lax.axis_index("seq"), counts[0]
    blk = q_ref.shape[0]
    width = own.shape[1]
    nk = kv.shape[1] // 2
    groups = nk // HD
    heads = q_ref.shape[1] // HD
    copies = [
        pltpu.make_async_copy(w_ref.at[:, columns_of(turn, width)], held.at[at], sems.at[at])
        for at, turn in enumerate(ORDER)
    ]
    start_all(copies)
    half = blk // 2
    key = lax.broadcasted_iota(jnp.int32, (blk, blk), 0)
    row = lax.broadcasted_iota(jnp.int32, (blk, blk), 1) % half
    own_seen = [(key <= row + at * half) & (key < count) for at in range(2)]
    front = jnp.zeros((blk, blk), jnp.int32) + seq > 0
    nq = q_ref.shape[1]
    for g in range(groups):
        kc, vc = pl.ds(g * HD, HD), pl.ds(nk + g * HD, HD)
        ac, bc = pl.ds(nq + g * HD, HD), pl.ds(nq + nk + g * HD, HD)
        ka = jnp.concatenate([a_mine[:, ac], a_other[:, kc]], axis=0)
        va = jnp.concatenate([a_mine[:, bc], a_other[:, vc]], axis=0)
        va = va.astype(jnp.float32)
        va = jnp.where(va == va, va, 0.0).astype(kv.dtype)
        keys = jnp.concatenate([ka, kv[:blk, kc]], axis=0)
        values = jnp.concatenate([va, kv[:blk, vc]], axis=0).T
        valid = None
        for h in range(g * (heads // groups), (g + 1) * (heads // groups), 2):
            for at in range(2):
                rows = pl.ds(at * half, half)
                size = blk + (at + 1) * half
                q = jnp.concatenate([q_ref[rows, pl.ds((h + i) * HD, HD)] for i in range(2)], axis=0)
                s = score_dot(keys[:size], q)
                if valid is None:
                    valid = front & (s[:blk] == s[:blk])
                seen = jnp.concatenate([valid, own_seen[at][: size - blk]], axis=0)
                s = jnp.where(seen, s, NEG)
                p = jnp.exp2((s - jnp.max(s, axis=0, keepdims=True)) * LOG2_SCALE)
                p = p * (1.0 / jnp.sum(p, axis=0, keepdims=True))
                o = exact_dot(values[:, :size], p.astype(kv.dtype)).T.astype(ctx.dtype)
                for i in range(2):
                    ctx[rows, pl.ds((h + i) * HD, HD)] = o[i * half : (i + 1) * half]
    for at in range(4):
        copies[at].wait()
        part = exact_dot(ctx[...], held[at])
        ref = (out0, out1, out2, own)[at]
        ref[...] = part.astype(ref.dtype)


def context(counts, q, kv, a_mine, a_other, w_out):
    blk, nq = q.shape
    depth, wide = w_out.shape
    width = wide // 4
    return pl.pallas_call(
        context_kernel,
        in_specs=[SMEM] + [VMEM] * 4 + [HBM],
        out_specs=[VMEM] * 4,
        out_shape=[jax.ShapeDtypeStruct((blk, width), q.dtype)] * 3
        + [jax.ShapeDtypeStruct((blk, width), jnp.float32)],
        scratch_shapes=[
            pltpu.VMEM((blk, nq), q.dtype),
            pltpu.VMEM((4, depth, width), q.dtype),
            pltpu.SemaphoreType.DMA((4,)),
        ],
        compiler_params=params(),
        cost_estimate=cost(4 * blk * 512 * nq + 2 * blk * depth * wide, 12 * MIB),
    )(counts, q, kv, a_mine, a_other, w_out)


def merge_kernel(parts, w_ref, out0, out1, out2, out3, held, sems):
    width = out0.shape[1]
    heads = (parts.shape[2] - HD) // HD
    copies = [
        pltpu.make_async_copy(w_ref.at[:, columns_of(at, width)], held.at[at], sems.at[at])
        for at in range(4)
    ]
    start_all(copies)
    stats = parts[:, :, pl.ds(heads * HD, HD)].astype(jnp.float32)
    stats = [stats[:, :, i * heads : (i + 1) * heads] for i in range(6)]
    m = stats[0] + stats[1] + stats[2]
    t = stats[3] + stats[4] + stats[5]
    scale = jnp.exp2((m - jnp.max(m, axis=0, keepdims=True)) * LOG2_SCALE)
    total = jnp.sum(scale * t, axis=0)
    ctx = []
    for h in range(heads):
        o = parts[:, :, pl.ds(h * HD, HD)].astype(jnp.float32)
        ctx.append(jnp.sum(scale[:, :, h : h + 1] * o, axis=0) / total[:, h : h + 1])
    ctx = jnp.concatenate(ctx, axis=1).astype(w_ref.dtype)
    for at in range(4):
        copies[at].wait()
        (out0, out1, out2, out3)[at][...] = exact_dot(ctx, held[at])


def merge(parts, w_out):
    slab = parts.shape[1]
    depth, wide = w_out.shape
    width = wide // 4
    return pl.pallas_call(
        merge_kernel,
        in_specs=[VMEM, HBM],
        out_specs=[VMEM] * 4,
        out_shape=[jax.ShapeDtypeStruct((slab, width), jnp.float32)] * 4,
        scratch_shapes=[
            pltpu.VMEM((4, depth, width), w_out.dtype),
            pltpu.SemaphoreType.DMA((4,)),
        ],
        compiler_params=params(),
        cost_estimate=cost(2 * 128 * depth * wide, depth * wide * 2),
    )(parts, w_out)


def total_kernel(a, b, c, d, out):
    total = (a[...] + b[...]) + (c[...] + d[...])
    total = jnp.concatenate([total, total], axis=0).astype(out.dtype)
    for at in range(0, out.shape[0], total.shape[0]):
        out[pl.ds(at, total.shape[0]), :] = total


def local(tokens, queries, valid_counts, query_host, w_query, w_key, w_value, w_out):
    host = query_host[0]
    blk, width = tokens.shape
    slab = blk // (2 * PAIRS)
    dtype = tokens.dtype
    half = blk // 2
    right, left = head_shift(tokens, 1), head_shift(tokens, 3)
    sibling = core_swap(valid_counts)

    sent = lax.cond(
        host == 0,
        lambda q, t: choose(valid_counts, core_swap(q), t),
        lambda q, t: choose(valid_counts, q, t),
        queries,
        tokens,
    )
    source = (jnp.maximum(host, 1) * slab).astype(jnp.uint32)
    sent, source = lax.optimization_barrier((sent, source))
    spread = lax.all_to_all(sent, "seq", 0, 0, tiled=True)
    zero = jnp.zeros_like(source)
    picked = jnp.concatenate(
        [lax.dynamic_slice(spread, (source, zero), (slab, width)), spread[:slab]], axis=0
    )
    picked, sibling = lax.optimization_barrier((picked, sibling))
    copies = jnp.broadcast_to(picked[None], (4,) + picked.shape)
    fews = lax.all_to_all(copies, "head", 0, 0, tiled=True)
    right_half, left_half, _ = lax.optimization_barrier((right[:half], left[half:], picked))
    chunks = [tokens, right, head_shift(right_half, 1), head_shift(left_half, 3), left]
    pack, few_kv = project_few(fews, w_query, w_key, w_value)
    mine = plane_swap(pack).reshape(blk // 2, -1)
    kv = project_keys(chunks, w_key, w_value, few_kv)
    kv_other = core_swap(kv)
    chunks[0], kv = lax.optimization_barrier((chunks[0], kv))
    q_blk = project_queries(chunks, w_query)
    mine, q_blk = lax.optimization_barrier((mine, q_blk))
    mine_other = core_swap(mine[:, w_query.shape[1] :])

    stats = query_attention(valid_counts, sibling, mine, kv, kv_other)
    merged = plane_swap(stats.reshape(PAIRS, slab, -1))
    *partial, own = context(valid_counts, q_blk, kv, mine, mine_other, w_out)
    far, after, before, own = context(valid_counts, q_blk, kv, mine, mine_other, w_out)
    merged, own, before, far = lax.optimization_barrier((merged, own, before, far))
    term = merge(merged, w_out)
    parts = [term[0]] + [head_shift(term[step], step) for step in (1, 2, 3)]
    before, _ = lax.optimization_barrier((before, term[0]))
    near = head_shift(after, 1), head_shift(before, 3)
    copies = pl.pallas_call(
        total_kernel,
        out_shape=jax.ShapeDtypeStruct((blk, width), dtype),
        compiler_params=params(24),
    )(*parts)
    far, copies = lax.optimization_barrier((far, copies))
    far = head_shift(far, 2)
    query_out = lax.all_to_all(copies, "seq", 0, 0, tiled=True)
    block_sum = own
    for part in (*near, far):
        block_sum += part.astype(jnp.float32)
    return (block_sum.astype(dtype), query_out)


def solution(mesh):
    return jax.shard_map(
        local,
        mesh=mesh,
        in_specs=(
            P("seq", "head"),
            P("seq", "head"),
            P("seq"),
            P(),
            P(None, "head"),
            P(None, "head"),
            P(None, "head"),
            P("head", None),
        ),
        out_specs=(P("seq", "head"), P(None, "head")),
        check_vma=False,
    )
```

profile of v0, /device:TPU:14, one launch (start us, length us, event | category | flops | bytes accessed | tf_op | source)
XLA Modules:
  0.0 108.3 jit_solution(16097422887325688031)
XLA Ops:
  1.3 2.5 %conditional.1 = (bf16[256,1024]{1,0:T(8,128)(2,1)}) conditional(s32[]{:T(128)} %bitcast, (s32[1]{0:T(128)}, bf16[256,1024]{1,0:T(8,128)(2,1)}, bf16[256,1024]{1,0:T(8,128)(2,1)}) %tuple.22, (bf16[256,1024]{1,0:T(8,128)(2,1)}, s32[1]{0:T(128)}, bf16[256,1024]{1,0:T(8,128)(2,1)}) %tuple.23), branch_computations={%region_0.0_spmd, %region_1.0_spmd} | conditional | flops 1000 | bytes 4194352 | solution.py:450
  1.3 2.5 %branch_0_fun.1 = bf16[256,1024]{1,0:T(8,128)(2,1)} custom-call(s32[1]{0:T(128)} %get-tuple-element.8.counts, bf16[256,1024]{1,0:T(8,128)(2,1)} %get-tuple-element.16.queries, bf16[256,1024]{1,0:T(8,128)(2,1)} %get-tuple-element.17.tokens), custom_call_target="tpu_custom_call" | custom-call | flops 1000 | bytes 2097152 | tf_op jit(solution)/shard_map/cond/branch_0_fun/pallas_call | solution.py:67
  3.8 8.7 %all-to-all-start = ((bf16[32,8,1024]{2,1,0:T(8,128)(2,1)}), bf16[32,8,1024]{2,1,0:T(8,128)(2,1)S(1)}, u32[]{:S(2)}, u32[]{:S(2)}) async-start(bf16[32,8,1024]{2,1,0:T(8,128)(2,1)} %bitcast.2), calls=%async_computation | async-start | bytes 1048576 | tf_op jit(solution)/shard_map/all_to_all | solution.py:459
  13.1 1.5 %collective-permute-start.3 = (bf16[256,1024]{1,0:T(8,128)(2,1)}, bf16[256,1024]{1,0:T(8,128)(2,1)S(1)}, u32[]{:S(2)}, u32[]{:S(2)}) collective-permute-start(bf16[256,1024]{1,0:T(8,128)(2,1)} %refs_0_.2), channel_id=1, source_target_pairs={{0,3},{1,0},{2,1},{3,2},{4,7},{5,4},{6,5},{7,6},{8,11},{9,8},{10,9... | collective-permute-start | bytes 1572872 | tf_op jit(solution)/shard_map/ppermute | solution.py:38
  14.6 8.4 %all-to-all-done = bf16[32,8,1024]{2,1,0:T(8,128)(2,1)S(1)} async-done(((bf16[32,8,1024]{2,1,0:T(8,128)(2,1)}), bf16[32,8,1024]{2,1,0:T(8,128)(2,1)S(1)}, u32[]{:S(2)}, u32[]{:S(2)}) %all-to-all-start) | async-done | bytes 524320 | tf_op jit(solution)/shard_map/all_to_all | solution.py:459
  23.7 4.8 %all-to-all-start.1 = ((bf16[4,16,1024]{2,1,0:T(8,128)(2,1)}), bf16[4,16,1024]{2,1,0:T(8,128)(2,1)S(1)}, u32[]{:S(2)}, u32[]{:S(2)}) async-start(bf16[4,16,1024]{2,1,0:T(8,128)(2,1)} %broadcast_in_dim.2), calls=%async_computation.1 | async-start | bytes 262144 | tf_op jit(solution)/shard_map/all_to_all | solution.py:466
  28.7 2.0 %collective-permute-start.5 = (bf16[128,1024]{1,0:T(8,128)(2,1)S(1)}, bf16[128,1024]{1,0:T(8,128)(2,1)S(1)}, u32[]{:S(2)}, u32[]{:S(2)}) collective-permute-start(bf16[128,1024]{1,0:T(8,128)(2,1)S(1)} %slice.22), channel_id=1, source_target_pairs={{0,3},{1,0},{2,1},{3,2},{4,7},{5,4},{6,5},{7,6},{8,11},{9,8},{10,9... | collective-permute-start | bytes 786440 | tf_op jit(solution)/shard_map/ppermute | solution.py:38
  30.7 2.0 %all-to-all-done.1.fews = bf16[4,16,1024]{2,1,0:T(8,128)(2,1)S(1)} async-done(((bf16[4,16,1024]{2,1,0:T(8,128)(2,1)}), bf16[4,16,1024]{2,1,0:T(8,128)(2,1)S(1)}, u32[]{:S(2)}, u32[]{:S(2)}) %all-to-all-start.1) | async-done | bytes 131104 | tf_op jit(solution)/shard_map/all_to_all | solution.py:466
  32.7 5.9 %shard_map.95 = (bf16[16,8,1536]{2,1,0:T(8,128)(2,1)}, bf16[16,512]{1,0:T(8,128)(2,1)S(1)}) custom-call(bf16[4,16,1024]{2,1,0:T(8,128)(2,1)S(1)} %all-to-all-done.1.fews, bf16[4096,1024]{1,0:T(8,128)(2,1)} %refs_5_.3, bf16[4096,256]{1,0:T(8,128)(2,1)} %refs_5_.2, bf16[4096,256]{1,0:T(8,128)(2,1)} %refs_6_.1), custom_call_target="tpu_custom_call" | custom-call | flops 1610612736 | bytes 12582912 | tf_op jit(solution)/shard_map/pallas_call | solution.py:123
  38.6 5.6 %all-to-all-start.2 = ((bf16[16,8,1536]{2,1,0:T(8,128)(2,1)}), bf16[16,8,1536]{2,1,0:T(8,128)(2,1)S(1)}, u32[]{:S(2)}, u32[]{:S(2)}) async-start(bf16[16,8,1536]{2,1,0:T(8,128)(2,1)} %get-tuple-element.54), calls=%async_computation.2 | async-start | bytes 786432 | tf_op jit(solution)/shard_map/all_to_all | solution.py:30
  44.2 2.8 %shard_map.96.mine.kv = bf16[272,512]{1,0:T(8,128)(2,1)S(1)} custom-call(bf16[256,1024]{1,0:T(8,128)(2,1)S(1)} %copy-done.2, bf16[256,1024]{1,0:T(8,128)(2,1)S(1)} %collective-permute-done.2.refs_1_, bf16[128,1024]{1,0:T(8,128)(2,1)S(1)} %collective-permute-done.4.refs_2_, bf16[128,1024]{1,0:T(8,128)(2,1)S(1)} %collective-permute-done.5.refs_3_, ...), custom_call_target="tpu_custom_call" | custom-call | flops 1073741824 | bytes 6291456 | tf_op jit(solution)/shard_map/pallas_call | solution.py:186
  47.1 4.3 %shard_map.97.q_ref = bf16[256,1024]{1,0:T(8,128)(2,1)S(1)} custom-call(bf16[256,1024]{1,0:T(8,128)(2,1)S(1)} %copy-done.2, bf16[256,1024]{1,0:T(8,128)(2,1)S(1)} %collective-permute-done.2.refs_1_, bf16[128,1024]{1,0:T(8,128)(2,1)S(1)} %collective-permute-done.4.refs_2_, bf16[128,1024]{1,0:T(8,128)(2,1)S(1)} %collective-permute-done.5.refs_3_, ...), custom_call_target="tpu_custom_call" | custom-call | flops 2147483648 | bytes 10485760 | tf_op jit(solution)/shard_map/pallas_call | solution.py:233
  53.0 3.3 %shard_map.98 = bf16[128,1152]{1,0:T(8,128)(2,1)} custom-call(s32[1]{0:T(128)S(6)} %copy.13.counts, s32[1]{0:T(128)} %collective-permute-done.1.sibling, bf16[128,1536]{1,0:T(8,128)(2,1)S(1)} %bitcast.11, bf16[272,512]{1,0:T(8,128)(2,1)S(1)} %shard_map.96.mine.kv, bf16[272,512]{1,0:T(8,128)(2,1)S(1)} %collective-permute-done.6.other), custom_call_target="tpu_custom_call" | custom-call | flops 335544320 | bytes 4194304 | tf_op jit(solution)/shard_map/pallas_call | solution.py:303
  56.3 7.0 %all-to-all-start.3 = ((bf16[16,8,1152]{2,1,0:T(8,128)(2,1)}), bf16[16,8,1152]{2,1,0:T(8,128)(2,1)S(1)}, u32[]{:S(2)}, u32[]{:S(2)}) async-start(bf16[16,8,1152]{2,1,0:T(8,128)(2,1)} %bitcast.6), calls=%async_computation.3 | async-start | bytes 589824 | tf_op jit(solution)/shard_map/all_to_all | solution.py:30
  63.3 8.9 %shard_map.99 = (bf16[256,1024]{1,0:T(8,128)(2,1)S(1)}, bf16[256,1024]{1,0:T(8,128)(2,1)S(1)}, bf16[256,1024]{1,0:T(8,128)(2,1)}, f32[256,1024]{1,0:T(8,128)}) custom-call(s32[1]{0:T(128)S(6)} %copy.13.counts, bf16[256,1024]{1,0:T(8,128)(2,1)} %copy-done.1, bf16[272,512]{1,0:T(8,128)(2,1)S(1)} %shard_map.96.mine.kv, bf16[128,1536]{1,0:T(8,128)(2,1)S(1)} %bitcast.12, ...), custom_call_target="tpu_custom_call" | custom-call | flops 2684354560 | bytes 12582912 | tf_op jit(solution)/shard_map/pallas_call | solution.py:376
  72.3 4.1 %shard_map.100 = (f32[8,1024]{1,0:T(8,128)S(1)}, f32[8,1024]{1,0:T(8,128)S(1)}, f32[8,1024]{1,0:T(8,128)S(1)}, f32[8,1024]{1,0:T(8,128)S(1)}) custom-call(bf16[16,8,1152]{2,1,0:T(8,128)(2,1)S(1)} %all-to-all-done.3.parts, bf16[1024,4096]{1,0:T(8,128)(2,1)} %w_ref.3), custom_call_target="tpu_custom_call" | custom-call | flops 1073741824 | bytes 8388608 | tf_op jit(solution)/shard_map/pallas_call | solution.py:420
  76.4 1.8 %collective-permute-start.10 = (f32[8,1024]{1,0:T(8,128)S(1)}, f32[8,1024]{1,0:T(8,128)S(1)}, u32[]{:S(2)}, u32[]{:S(2)}) collective-permute-start(f32[8,1024]{1,0:T(8,128)S(1)} %get-tuple-element.72), channel_id=1, source_target_pairs={{0,1},{1,2},{2,3},{3,0},{4,5},{5,6},{6,7},{7,4},{8,9},{9,10},{10,1... | collective-permute-start | bytes 98312 | tf_op jit(solution)/shard_map/ppermute | solution.py:38
  78.5 1.0 collective-permute-start.12
  79.5 2.3 %collective-permute-start.8 = (bf16[256,1024]{1,0:T(8,128)(2,1)S(1)}, bf16[256,1024]{1,0:T(8,128)(2,1)S(1)}, u32[]{:S(2)}, u32[]{:S(2)}) collective-permute-start(bf16[256,1024]{1,0:T(8,128)(2,1)S(1)} %get-tuple-element.66), channel_id=1, source_target_pairs={{0,1},{1,2},{2,3},{3,0},{4,5},{5,6},{6,7},{7,4},{8,9},{9,10},{10,1... | collective-permute-start | bytes 1572872 | tf_op jit(solution)/shard_map/ppermute | solution.py:38
  81.8 1.9 %collective-permute-done.11.c = f32[8,1024]{1,0:T(8,128)S(1)} collective-permute-done((f32[8,1024]{1,0:T(8,128)S(1)}, f32[8,1024]{1,0:T(8,128)S(1)}, u32[]{:S(2)}, u32[]{:S(2)}) %collective-permute-start.11) | collective-permute-done | bytes 32800 | tf_op jit(solution)/shard_map/ppermute | solution.py:38
  84.0 2.0 %collective-permute-start.13 = (bf16[256,1024]{1,0:T(8,128)(2,1)S(1)}, bf16[256,1024]{1,0:T(8,128)(2,1)S(1)}, u32[]{:S(2)}, u32[]{:S(2)}) collective-permute-start(bf16[256,1024]{1,0:T(8,128)(2,1)S(1)} %get-tuple-element.75), channel_id=1, source_target_pairs={{0,2},{1,3},{2,0},{3,1},{4,6},{5,7},{6,4},{7,5},{8,10},{9,11},{10,... | collective-permute-start | bytes 1572872 | tf_op jit(solution)/shard_map/ppermute | solution.py:38
  86.1 17.7 %all_to_all.39 = bf16[32,8,1024]{2,1,0:T(8,128)(2,1)S(1)} all-to-all(bf16[32,8,1024]{2,1,0:T(8,128)(2,1)S(1)} %bitcast.13), channel_id=1, replica_groups=mesh['seq'=32,'head'=4] {'seq'}, dimensions={0} | all-to-all | bytes 1048576 | tf_op jit(solution)/shard_map/all_to_all | solution.py:494
  103.7 2.7 %collective-permute-done.13 = bf16[256,1024]{1,0:T(8,128)(2,1)S(1)} collective-permute-done((bf16[256,1024]{1,0:T(8,128)(2,1)S(1)}, bf16[256,1024]{1,0:T(8,128)(2,1)S(1)}, u32[]{:S(2)}, u32[]{:S(2)}) %collective-permute-start.13) | collective-permute-done | bytes 524320 | tf_op jit(solution)/shard_map/ppermute | solution.py:38
  106.4 1.1 %add_convert_fusion = bf16[256,1024]{1,0:T(8,128)(2,1)} fusion(bf16[256,1024]{1,0:T(8,128)(2,1)S(1)} %collective-permute-done.13, bf16[256,1024]{1,0:T(8,128)(2,1)S(1)} %collective-permute-done.9, f32[256,1024]{1,0:T(8,128)S(1)} %copy-done.3, bf16[256,1024]{1,0:T(8,128)(2,1)S(1)} %collective-permute-done.8), kind=kLoop, calls=%fused_computation | loop fusion | flops 1835008 | bytes 3145728 | tf_op jit(solution)/shard_map/convert_element_type | solution.py:498
  (39 shorter events, 3.8 us)
Async XLA Ops:
  3.8 40.4 %copy-start.2 = (bf16[256,1024]{1,0:T(8,128)(2,1)S(1)}, bf16[256,1024]{1,0:T(8,128)(2,1)}, u32[]{:S(2)}) copy-start(bf16[256,1024]{1,0:T(8,128)(2,1)} %refs_0_.2) | copy-start | bytes 1572868
  3.8 19.2 %all-to-all-start = ((bf16[32,8,1024]{2,1,0:T(8,128)(2,1)}), bf16[32,8,1024]{2,1,0:T(8,128)(2,1)S(1)}, u32[]{:S(2)}, u32[]{:S(2)}) async-start(bf16[32,8,1024]{2,1,0:T(8,128)(2,1)} %bitcast.2), calls=%async_computation | async-start | bytes 1048576 | tf_op jit(solution)/shard_map/all_to_all | solution.py:459
  12.5 16.0 %collective-permute-start.2 = (bf16[256,1024]{1,0:T(8,128)(2,1)}, bf16[256,1024]{1,0:T(8,128)(2,1)S(1)}, u32[]{:S(2)}, u32[]{:S(2)}) collective-permute-start(bf16[256,1024]{1,0:T(8,128)(2,1)} %refs_0_.2), channel_id=1, source_target_pairs={{0,1},{1,2},{2,3},{3,0},{4,5},{5,6},{6,7},{7,4},{8,9},{9,10},{10,1... | collective-permute-start | bytes 1572872 | tf_op jit(solution)/shard_map/ppermute | solution.py:38
  13.1 15.5 %collective-permute-start.3 = (bf16[256,1024]{1,0:T(8,128)(2,1)}, bf16[256,1024]{1,0:T(8,128)(2,1)S(1)}, u32[]{:S(2)}, u32[]{:S(2)}) collective-permute-start(bf16[256,1024]{1,0:T(8,128)(2,1)} %refs_0_.2), channel_id=1, source_target_pairs={{0,3},{1,0},{2,1},{3,2},{4,7},{5,4},{6,5},{7,6},{8,11},{9,8},{10,9... | collective-permute-start | bytes 1572872 | tf_op jit(solution)/shard_map/ppermute | solution.py:38
  14.6 8.4 %collective-permute-start.1 = (s32[1]{0:T(128)}, s32[1]{0:T(128)}, u32[]{:S(2)}, u32[]{:S(2)}) collective-permute-start(s32[1]{0:T(128)} %param.12), channel_id=1, source_target_pairs={{0,4},{4,0},{8,12},{12,8},{16,20},{20,16},{24,28},{28,24},{32,36},... | collective-permute-start | bytes 20 | tf_op jit(solution)/shard_map/ppermute | solution.py:34
  23.7 9.0 %all-to-all-start.1 = ((bf16[4,16,1024]{2,1,0:T(8,128)(2,1)}), bf16[4,16,1024]{2,1,0:T(8,128)(2,1)S(1)}, u32[]{:S(2)}, u32[]{:S(2)}) async-start(bf16[4,16,1024]{2,1,0:T(8,128)(2,1)} %broadcast_in_dim.2), calls=%async_computation.1 | async-start | bytes 262144 | tf_op jit(solution)/shard_map/all_to_all | solution.py:466
  28.6 18.5 %copy-start = (bf16[256,1024]{1,0:T(8,128)(2,1)}, bf16[256,1024]{1,0:T(8,128)(2,1)S(1)}, u32[]{:S(2)}) copy-start(bf16[256,1024]{1,0:T(8,128)(2,1)S(1)} %collective-permute-done.3.refs_4_) | copy-start | bytes 1572868
  28.6 15.6 %collective-permute-start.4 = (bf16[128,1024]{1,0:T(8,128)(2,1)S(1)}, bf16[128,1024]{1,0:T(8,128)(2,1)S(1)}, u32[]{:S(2)}, u32[]{:S(2)}) collective-permute-start(bf16[128,1024]{1,0:T(8,128)(2,1)S(1)} %slice.21), channel_id=1, source_target_pairs={{0,1},{1,2},{2,3},{3,0},{4,5},{5,6},{6,7},{7,4},{8,9},{9,10},{10,1... | collective-permute-start | bytes 786440 | tf_op jit(solution)/shard_map/ppermute | solution.py:38
  28.7 15.5 %collective-permute-start.5 = (bf16[128,1024]{1,0:T(8,128)(2,1)S(1)}, bf16[128,1024]{1,0:T(8,128)(2,1)S(1)}, u32[]{:S(2)}, u32[]{:S(2)}) collective-permute-start(bf16[128,1024]{1,0:T(8,128)(2,1)S(1)} %slice.22), channel_id=1, source_target_pairs={{0,3},{1,0},{2,1},{3,2},{4,7},{5,4},{6,5},{7,6},{8,11},{9,8},{10,9... | collective-permute-start | bytes 786440 | tf_op jit(solution)/shard_map/ppermute | solution.py:38
  38.6 13.6 %all-to-all-start.2 = ((bf16[16,8,1536]{2,1,0:T(8,128)(2,1)}), bf16[16,8,1536]{2,1,0:T(8,128)(2,1)S(1)}, u32[]{:S(2)}, u32[]{:S(2)}) async-start(bf16[16,8,1536]{2,1,0:T(8,128)(2,1)} %get-tuple-element.54), calls=%async_computation.2 | async-start | bytes 786432 | tf_op jit(solution)/shard_map/all_to_all | solution.py:30
  47.0 6.0 %collective-permute-start.6 = (bf16[272,512]{1,0:T(8,128)(2,1)S(1)}, bf16[272,512]{1,0:T(8,128)(2,1)S(1)}, u32[]{:S(2)}, u32[]{:S(2)}) collective-permute-start(bf16[272,512]{1,0:T(8,128)(2,1)S(1)} %shard_map.96.mine.kv), channel_id=1, source_target_pairs={{0,4},{4,0},{8,12},{12,8},{16,20},{20,16},{24,28},{28,24},{32,36},... | collective-permute-start | bytes 835592 | tf_op jit(solution)/shard_map/ppermute | solution.py:34
  51.5 11.8 %copy-start.1 = (bf16[256,1024]{1,0:T(8,128)(2,1)}, bf16[256,1024]{1,0:T(8,128)(2,1)S(1)}, u32[]{:S(2)}) copy-start(bf16[256,1024]{1,0:T(8,128)(2,1)S(1)} %shard_map.97.q_ref) | copy-start | bytes 1572868
  52.3 11.0 %collective-permute-start.7 = (bf16[128,512]{1,0:T(8,128)(2,1)S(1)}, bf16[128,512]{1,0:T(8,128)(2,1)S(1)}, u32[]{:S(2)}, u32[]{:S(2)}) collective-permute-start(bf16[128,512]{1,0:T(8,128)(2,1)S(1)} %slice.19), channel_id=1, source_target_pairs={{0,4},{4,0},{8,12},{12,8},{16,20},{20,16},{24,28},{28,24},{32,36},... | collective-permute-start | bytes 393224 | tf_op jit(solution)/shard_map/ppermute | solution.py:34
  56.3 15.9 %all-to-all-start.3 = ((bf16[16,8,1152]{2,1,0:T(8,128)(2,1)}), bf16[16,8,1152]{2,1,0:T(8,128)(2,1)S(1)}, u32[]{:S(2)}, u32[]{:S(2)}) async-start(bf16[16,8,1152]{2,1,0:T(8,128)(2,1)} %bitcast.6), calls=%async_computation.3 | async-start | bytes 589824 | tf_op jit(solution)/shard_map/all_to_all | solution.py:30
  72.2 9.5 %copy-start.4 = (bf16[256,1024]{1,0:T(8,128)(2,1)S(1)}, bf16[256,1024]{1,0:T(8,128)(2,1)}, u32[]{:S(2)}) copy-start(bf16[256,1024]{1,0:T(8,128)(2,1)} %get-tuple-element.70) | copy-start | bytes 1572868
  72.3 34.2 %copy-start.3 = (f32[256,1024]{1,0:T(8,128)S(1)}, f32[256,1024]{1,0:T(8,128)}, u32[]{:S(2)}) copy-start(f32[256,1024]{1,0:T(8,128)} %get-tuple-element.65) | copy-start | bytes 3145732
  76.4 5.4 %collective-permute-start.10 = (f32[8,1024]{1,0:T(8,128)S(1)}, f32[8,1024]{1,0:T(8,128)S(1)}, u32[]{:S(2)}, u32[]{:S(2)}) collective-permute-start(f32[8,1024]{1,0:T(8,128)S(1)} %get-tuple-element.72), channel_id=1, source_target_pairs={{0,1},{1,2},{2,3},{3,0},{4,5},{5,6},{6,7},{7,4},{8,9},{9,10},{10,1... | collective-permute-start | bytes 98312 | tf_op jit(solution)/shard_map/ppermute | solution.py:38
  78.2 5.5 %collective-permute-start.11 = (f32[8,1024]{1,0:T(8,128)S(1)}, f32[8,1024]{1,0:T(8,128)S(1)}, u32[]{:S(2)}, u32[]{:S(2)}) collective-permute-start(f32[8,1024]{1,0:T(8,128)S(1)} %get-tuple-element.73), channel_id=1, source_target_pairs={{0,2},{1,3},{2,0},{3,1},{4,6},{5,7},{6,4},{7,5},{8,10},{9,11},{10,... | collective-permute-start | bytes 98312 | tf_op jit(solution)/shard_map/ppermute | solution.py:38
  78.5 5.4 %collective-permute-start.12 = (f32[8,1024]{1,0:T(8,128)S(1)}, f32[8,1024]{1,0:T(8,128)S(1)}, u32[]{:S(2)}, u32[]{:S(2)}) collective-permute-start(f32[8,1024]{1,0:T(8,128)S(1)} %get-tuple-element.74), channel_id=1, source_target_pairs={{0,3},{1,0},{2,1},{3,2},{4,7},{5,4},{6,5},{7,6},{8,11},{9,8},{10,9... | collective-permute-start | bytes 98312 | tf_op jit(solution)/shard_map/ppermute | solution.py:38
  79.5 24.2 %collective-permute-start.8 = (bf16[256,1024]{1,0:T(8,128)(2,1)S(1)}, bf16[256,1024]{1,0:T(8,128)(2,1)S(1)}, u32[]{:S(2)}, u32[]{:S(2)}) collective-permute-start(bf16[256,1024]{1,0:T(8,128)(2,1)S(1)} %get-tuple-element.66), channel_id=1, source_target_pairs={{0,1},{1,2},{2,3},{3,0},{4,5},{5,6},{6,7},{7,4},{8,9},{9,10},{10,1... | collective-permute-start | bytes 1572872 | tf_op jit(solution)/shard_map/ppermute | solution.py:38
  81.8 22.0 %collective-permute-start.9 = (bf16[256,1024]{1,0:T(8,128)(2,1)S(1)}, bf16[256,1024]{1,0:T(8,128)(2,1)S(1)}, u32[]{:S(2)}, u32[]{:S(2)}) collective-permute-start(bf16[256,1024]{1,0:T(8,128)(2,1)S(1)} %copy-done.4), channel_id=1, source_target_pairs={{0,3},{1,0},{2,1},{3,2},{4,7},{5,4},{6,5},{7,6},{8,11},{9,8},{10,9... | collective-permute-start | bytes 1572872 | tf_op jit(solution)/shard_map/ppermute | solution.py:38
  84.0 22.4 %collective-permute-start.13 = (bf16[256,1024]{1,0:T(8,128)(2,1)S(1)}, bf16[256,1024]{1,0:T(8,128)(2,1)S(1)}, u32[]{:S(2)}, u32[]{:S(2)}) collective-permute-start(bf16[256,1024]{1,0:T(8,128)(2,1)S(1)} %get-tuple-element.75), channel_id=1, source_target_pairs={{0,2},{1,3},{2,0},{3,1},{4,6},{5,7},{6,4},{7,5},{8,10},{9,11},{10,... | collective-permute-start | bytes 1572872 | tf_op jit(solution)/shard_map/ppermute | solution.py:38
where the time goes:
time: 109 us; the launch traced here: 108 us
  starting transfers between devices  37.8 us (35%)
  Pallas kernels  32 us (29%)
  blocking collectives  17.7 us (16%)
  waiting for transfers between devices  16.1 us (15%)
  between operations  2.18 us (2%)
  local copies, waits for them, and re-layouts  1.55 us (1%)
  other arithmetic  1.12 us (1%)
    all_to_all x1, blocking collectives, local(): query_out = lax.all_to_all(copies, 'seq', 0, 0, tiled=True)  17.7 us
    all_to_all x2, starting transfers between devices, plane_swap(): lax.all_to_all(blocks, 'seq', 0, 0, axis_index_groups=PLANE, tiled=True)  12.5 us
    ppermute x10, starting transfers between devices, head_shift(): return lax.ppermute(block, 'head', [(i, (i + step) % 4) for i in range(4)])  11.6 us
    pallas_call x1, Pallas kernels, context(): pl.pallas_call(context_kernel, in_specs=[SMEM] + [VMEM] * 4 + [HBM], out_...  8.93 us
    all_to_all x1, starting transfers between devices, local(): spread = lax.all_to_all(sent, 'seq', 0, 0, tiled=True)  8.69 us
    all_to_all x1, waiting for transfers between devices, local(): spread = lax.all_to_all(sent, 'seq', 0, 0, tiled=True)  8.4 us
    pallas_call x1, Pallas kernels, project_few(): pl.pallas_call(few_kernel, in_specs=[VMEM] + [HBM] * 3, out_specs=[VMEM]...  5.94 us
    ppermute x10, waiting for transfers between devices, head_shift(): return lax.ppermute(block, 'head', [(i, (i + step) % 4) for i in range(4)])  4.93 us
  transfers between devices with their start and end apart: 17, of which 6 were waited for; matrix products, arithmetic and copies ran while one was open for 1% of the time, Pallas kernels for 23%

commit v1 on v0

--- a/solution.py
+++ b/solution.py
@@ -477,7 +477,6 @@
 
     stats = query_attention(valid_counts, sibling, mine, kv, kv_other)
     merged = plane_swap(stats.reshape(PAIRS, slab, -1))
-    *partial, own = context(valid_counts, q_blk, kv, mine, mine_other, w_out)
     far, after, before, own = context(valid_counts, q_blk, kv, mine, mine_other, w_out)
     merged, own, before, far = lax.optimization_barrier((merged, own, before, far))
     term = merge(merged, w_out)

time: 109 us -> 109 us (level)
  no operation moved by 1% of the time
where the time goes in v1:
time: 109 us; the launch traced here: 108 us
  starting transfers between devices  37.8 us (35%)
  Pallas kernels  32 us (29%)
  blocking collectives  17.7 us (16%)
  waiting for transfers between devices  16.1 us (15%)
  between operations  2.18 us (2%)
  local copies, waits for them, and re-layouts  1.55 us (1%)
  other arithmetic  1.12 us (1%)
    all_to_all x1, blocking collectives, local(): query_out = lax.all_to_all(copies, 'seq', 0, 0, tiled=True)  17.7 us
    all_to_all x2, starting transfers between devices, plane_swap(): lax.all_to_all(blocks, 'seq', 0, 0, axis_index_groups=PLANE, tiled=True)  12.5 us
    ppermute x10, starting transfers between devices, head_shift(): return lax.ppermute(block, 'head', [(i, (i + step) % 4) for i in range(4)])  11.6 us
    pallas_call x1, Pallas kernels, context(): pl.pallas_call(context_kernel, in_specs=[SMEM] + [VMEM] * 4 + [HBM], out_...  8.93 us
    all_to_all x1, starting transfers between devices, local(): spread = lax.all_to_all(sent, 'seq', 0, 0, tiled=True)  8.69 us
    all_to_all x1, waiting for transfers between devices, local(): spread = lax.all_to_all(sent, 'seq', 0, 0, tiled=True)  8.4 us
    pallas_call x1, Pallas kernels, project_few(): pl.pallas_call(few_kernel, in_specs=[VMEM] + [HBM] * 3, out_specs=[VMEM]...  5.94 us
    ppermute x10, waiting for transfers between devices, head_shift(): return lax.ppermute(block, 'head', [(i, (i + step) % 4) for i in range(4)])  4.93 us
  transfers between devices with their start and end apart: 17, of which 6 were waited for; matrix products, arithmetic and copies ran while one was open for 1% of the time, Pallas kernels for 23%

profile of v1, /device:TPU:14, one launch (start us, length us, event | category | flops | bytes accessed | tf_op | source)
XLA Modules:
  0.0 108.3 jit_solution(16097422887325688031)
XLA Ops:
  1.3 2.5 %conditional.1 = (bf16[256,1024]{1,0:T(8,128)(2,1)}) conditional(s32[]{:T(128)} %bitcast, (s32[1]{0:T(128)}, bf16[256,1024]{1,0:T(8,128)(2,1)}, bf16[256,1024]{1,0:T(8,128)(2,1)}) %tuple.22, (bf16[256,1024]{1,0:T(8,128)(2,1)}, s32[1]{0:T(128)}, bf16[256,1024]{1,0:T(8,128)(2,1)}) %tuple.23), branch_computations={%region_0.0_spmd, %region_1.0_spmd} | conditional | flops 1000 | bytes 4194352 | solution.py:450
  1.3 2.5 %branch_0_fun.1 = bf16[256,1024]{1,0:T(8,128)(2,1)} custom-call(s32[1]{0:T(128)} %get-tuple-element.8.counts, bf16[256,1024]{1,0:T(8,128)(2,1)} %get-tuple-element.16.queries, bf16[256,1024]{1,0:T(8,128)(2,1)} %get-tuple-element.17.tokens), custom_call_target="tpu_custom_call" | custom-call | flops 1000 | bytes 2097152 | tf_op jit(solution)/shard_map/cond/branch_0_fun/pallas_call | solution.py:67
  3.8 8.7 %all-to-all-start = ((bf16[32,8,1024]{2,1,0:T(8,128)(2,1)}), bf16[32,8,1024]{2,1,0:T(8,128)(2,1)S(1)}, u32[]{:S(2)}, u32[]{:S(2)}) async-start(bf16[32,8,1024]{2,1,0:T(8,128)(2,1)} %bitcast.2), calls=%async_computation | async-start | bytes 1048576 | tf_op jit(solution)/shard_map/all_to_all | solution.py:459
  13.1 1.5 %collective-permute-start.3 = (bf16[256,1024]{1,0:T(8,128)(2,1)}, bf16[256,1024]{1,0:T(8,128)(2,1)S(1)}, u32[]{:S(2)}, u32[]{:S(2)}) collective-permute-start(bf16[256,1024]{1,0:T(8,128)(2,1)} %refs_0_.2), channel_id=1, source_target_pairs={{0,3},{1,0},{2,1},{3,2},{4,7},{5,4},{6,5},{7,6},{8,11},{9,8},{10,9... | collective-permute-start | bytes 1572872 | tf_op jit(solution)/shard_map/ppermute | solution.py:38
  14.6 8.4 %all-to-all-done = bf16[32,8,1024]{2,1,0:T(8,128)(2,1)S(1)} async-done(((bf16[32,8,1024]{2,1,0:T(8,128)(2,1)}), bf16[32,8,1024]{2,1,0:T(8,128)(2,1)S(1)}, u32[]{:S(2)}, u32[]{:S(2)}) %all-to-all-start) | async-done | bytes 524320 | tf_op jit(solution)/shard_map/all_to_all | solution.py:459
  23.7 4.8 %all-to-all-start.1 = ((bf16[4,16,1024]{2,1,0:T(8,128)(2,1)}), bf16[4,16,1024]{2,1,0:T(8,128)(2,1)S(1)}, u32[]{:S(2)}, u32[]{:S(2)}) async-start(bf16[4,16,1024]{2,1,0:T(8,128)(2,1)} %broadcast_in_dim.2), calls=%async_computation.1 | async-start | bytes 262144 | tf_op jit(solution)/shard_map/all_to_all | solution.py:466
  28.7 2.0 %collective-permute-start.5 = (bf16[128,1024]{1,0:T(8,128)(2,1)S(1)}, bf16[128,1024]{1,0:T(8,128)(2,1)S(1)}, u32[]{:S(2)}, u32[]{:S(2)}) collective-permute-start(bf16[128,1024]{1,0:T(8,128)(2,1)S(1)} %slice.22), channel_id=1, source_target_pairs={{0,3},{1,0},{2,1},{3,2},{4,7},{5,4},{6,5},{7,6},{8,11},{9,8},{10,9... | collective-permute-start | bytes 786440 | tf_op jit(solution)/shard_map/ppermute | solution.py:38
  30.7 2.0 %all-to-all-done.1.fews = bf16[4,16,1024]{2,1,0:T(8,128)(2,1)S(1)} async-done(((bf16[4,16,1024]{2,1,0:T(8,128)(2,1)}), bf16[4,16,1024]{2,1,0:T(8,128)(2,1)S(1)}, u32[]{:S(2)}, u32[]{:S(2)}) %all-to-all-start.1) | async-done | bytes 131104 | tf_op jit(solution)/shard_map/all_to_all | solution.py:466
  32.7 5.9 %shard_map.95 = (bf16[16,8,1536]{2,1,0:T(8,128)(2,1)}, bf16[16,512]{1,0:T(8,128)(2,1)S(1)}) custom-call(bf16[4,16,1024]{2,1,0:T(8,128)(2,1)S(1)} %all-to-all-done.1.fews, bf16[4096,1024]{1,0:T(8,128)(2,1)} %refs_5_.3, bf16[4096,256]{1,0:T(8,128)(2,1)} %refs_5_.2, bf16[4096,256]{1,0:T(8,128)(2,1)} %refs_6_.1), custom_call_target="tpu_custom_call" | custom-call | flops 1610612736 | bytes 12582912 | tf_op jit(solution)/shard_map/pallas_call | solution.py:123
  38.6 5.6 %all-to-all-start.2 = ((bf16[16,8,1536]{2,1,0:T(8,128)(2,1)}), bf16[16,8,1536]{2,1,0:T(8,128)(2,1)S(1)}, u32[]{:S(2)}, u32[]{:S(2)}) async-start(bf16[16,8,1536]{2,1,0:T(8,128)(2,1)} %get-tuple-element.54), calls=%async_computation.2 | async-start | bytes 786432 | tf_op jit(solution)/shard_map/all_to_all | solution.py:30
  44.2 2.8 %shard_map.96.mine.kv = bf16[272,512]{1,0:T(8,128)(2,1)S(1)} custom-call(bf16[256,1024]{1,0:T(8,128)(2,1)S(1)} %copy-done.2, bf16[256,1024]{1,0:T(8,128)(2,1)S(1)} %collective-permute-done.2.refs_1_, bf16[128,1024]{1,0:T(8,128)(2,1)S(1)} %collective-permute-done.4.refs_2_, bf16[128,1024]{1,0:T(8,128)(2,1)S(1)} %collective-permute-done.5.refs_3_, ...), custom_call_target="tpu_custom_call" | custom-call | flops 1073741824 | bytes 6291456 | tf_op jit(solution)/shard_map/pallas_call | solution.py:186
  47.1 4.3 %shard_map.97.q_ref = bf16[256,1024]{1,0:T(8,128)(2,1)S(1)} custom-call(bf16[256,1024]{1,0:T(8,128)(2,1)S(1)} %copy-done.2, bf16[256,1024]{1,0:T(8,128)(2,1)S(1)} %collective-permute-done.2.refs_1_, bf16[128,1024]{1,0:T(8,128)(2,1)S(1)} %collective-permute-done.4.refs_2_, bf16[128,1024]{1,0:T(8,128)(2,1)S(1)} %collective-permute-done.5.refs_3_, ...), custom_call_target="tpu_custom_call" | custom-call | flops 2147483648 | bytes 10485760 | tf_op jit(solution)/shard_map/pallas_call | solution.py:233
  53.0 3.3 %shard_map.98 = bf16[128,1152]{1,0:T(8,128)(2,1)} custom-call(s32[1]{0:T(128)S(6)} %copy.13.counts, s32[1]{0:T(128)} %collective-permute-done.1.sibling, bf16[128,1536]{1,0:T(8,128)(2,1)S(1)} %bitcast.11, bf16[272,512]{1,0:T(8,128)(2,1)S(1)} %shard_map.96.mine.kv, bf16[272,512]{1,0:T(8,128)(2,1)S(1)} %collective-permute-done.6.other), custom_call_target="tpu_custom_call" | custom-call | flops 335544320 | bytes 4194304 | tf_op jit(solution)/shard_map/pallas_call | solution.py:303
  56.3 7.0 %all-to-all-start.3 = ((bf16[16,8,1152]{2,1,0:T(8,128)(2,1)}), bf16[16,8,1152]{2,1,0:T(8,128)(2,1)S(1)}, u32[]{:S(2)}, u32[]{:S(2)}) async-start(bf16[16,8,1152]{2,1,0:T(8,128)(2,1)} %bitcast.6), calls=%async_computation.3 | async-start | bytes 589824 | tf_op jit(solution)/shard_map/all_to_all | solution.py:30
  63.3 8.9 %shard_map.99 = (bf16[256,1024]{1,0:T(8,128)(2,1)S(1)}, bf16[256,1024]{1,0:T(8,128)(2,1)S(1)}, bf16[256,1024]{1,0:T(8,128)(2,1)}, f32[256,1024]{1,0:T(8,128)}) custom-call(s32[1]{0:T(128)S(6)} %copy.13.counts, bf16[256,1024]{1,0:T(8,128)(2,1)} %copy-done.1, bf16[272,512]{1,0:T(8,128)(2,1)S(1)} %shard_map.96.mine.kv, bf16[128,1536]{1,0:T(8,128)(2,1)S(1)} %bitcast.12, ...), custom_call_target="tpu_custom_call" | custom-call | flops 2684354560 | bytes 12582912 | tf_op jit(solution)/shard_map/pallas_call | solution.py:376
  72.3 4.1 %shard_map.100 = (f32[8,1024]{1,0:T(8,128)S(1)}, f32[8,1024]{1,0:T(8,128)S(1)}, f32[8,1024]{1,0:T(8,128)S(1)}, f32[8,1024]{1,0:T(8,128)S(1)}) custom-call(bf16[16,8,1152]{2,1,0:T(8,128)(2,1)S(1)} %all-to-all-done.3.parts, bf16[1024,4096]{1,0:T(8,128)(2,1)} %w_ref.3), custom_call_target="tpu_custom_call" | custom-call | flops 1073741824 | bytes 8388608 | tf_op jit(solution)/shard_map/pallas_call | solution.py:420
  76.4 1.8 %collective-permute-start.10 = (f32[8,1024]{1,0:T(8,128)S(1)}, f32[8,1024]{1,0:T(8,128)S(1)}, u32[]{:S(2)}, u32[]{:S(2)}) collective-permute-start(f32[8,1024]{1,0:T(8,128)S(1)} %get-tuple-element.72), channel_id=1, source_target_pairs={{0,1},{1,2},{2,3},{3,0},{4,5},{5,6},{6,7},{7,4},{8,9},{9,10},{10,1... | collective-permute-start | bytes 98312 | tf_op jit(solution)/shard_map/ppermute | solution.py:38
  78.5 1.0 collective-permute-start.12
  79.5 2.3 %collective-permute-start.8 = (bf16[256,1024]{1,0:T(8,128)(2,1)S(1)}, bf16[256,1024]{1,0:T(8,128)(2,1)S(1)}, u32[]{:S(2)}, u32[]{:S(2)}) collective-permute-start(bf16[256,1024]{1,0:T(8,128)(2,1)S(1)} %get-tuple-element.66), channel_id=1, source_target_pairs={{0,1},{1,2},{2,3},{3,0},{4,5},{5,6},{6,7},{7,4},{8,9},{9,10},{10,1... | collective-permute-start | bytes 1572872 | tf_op jit(solution)/shard_map/ppermute | solution.py:38
  81.8 1.9 %collective-permute-done.11.c = f32[8,1024]{1,0:T(8,128)S(1)} collective-permute-done((f32[8,1024]{1,0:T(8,128)S(1)}, f32[8,1024]{1,0:T(8,128)S(1)}, u32[]{:S(2)}, u32[]{:S(2)}) %collective-permute-start.11) | collective-permute-done | bytes 32800 | tf_op jit(solution)/shard_map/ppermute | solution.py:38
  84.0 2.0 %collective-permute-start.13 = (bf16[256,1024]{1,0:T(8,128)(2,1)S(1)}, bf16[256,1024]{1,0:T(8,128)(2,1)S(1)}, u32[]{:S(2)}, u32[]{:S(2)}) collective-permute-start(bf16[256,1024]{1,0:T(8,128)(2,1)S(1)} %get-tuple-element.75), channel_id=1, source_target_pairs={{0,2},{1,3},{2,0},{3,1},{4,6},{5,7},{6,4},{7,5},{8,10},{9,11},{10,... | collective-permute-start | bytes 1572872 | tf_op jit(solution)/shard_map/ppermute | solution.py:38
  86.1 17.7 %all_to_all.39 = bf16[32,8,1024]{2,1,0:T(8,128)(2,1)S(1)} all-to-all(bf16[32,8,1024]{2,1,0:T(8,128)(2,1)S(1)} %bitcast.13), channel_id=1, replica_groups=mesh['seq'=32,'head'=4] {'seq'}, dimensions={0} | all-to-all | bytes 1048576 | tf_op jit(solution)/shard_map/all_to_all | solution.py:493
  103.7 2.7 %collective-permute-done.13 = bf16[256,1024]{1,0:T(8,128)(2,1)S(1)} collective-permute-done((bf16[256,1024]{1,0:T(8,128)(2,1)S(1)}, bf16[256,1024]{1,0:T(8,128)(2,1)S(1)}, u32[]{:S(2)}, u32[]{:S(2)}) %collective-permute-start.13) | collective-permute-done | bytes 524320 | tf_op jit(solution)/shard_map/ppermute | solution.py:38
  106.4 1.1 %add_convert_fusion = bf16[256,1024]{1,0:T(8,128)(2,1)} fusion(bf16[256,1024]{1,0:T(8,128)(2,1)S(1)} %collective-permute-done.13, bf16[256,1024]{1,0:T(8,128)(2,1)S(1)} %collective-permute-done.9, f32[256,1024]{1,0:T(8,128)S(1)} %copy-done.3, bf16[256,1024]{1,0:T(8,128)(2,1)S(1)} %collective-permute-done.8), kind=kLoop, calls=%fused_computation | loop fusion | flops 1835008 | bytes 3145728 | tf_op jit(solution)/shard_map/convert_element_type | solution.py:497
  (39 shorter events, 3.8 us)
Async XLA Ops:
  3.8 40.4 %copy-start.2 = (bf16[256,1024]{1,0:T(8,128)(2,1)S(1)}, bf16[256,1024]{1,0:T(8,128)(2,1)}, u32[]{:S(2)}) copy-start(bf16[256,1024]{1,0:T(8,128)(2,1)} %refs_0_.2) | copy-start | bytes 1572868
  3.8 19.2 %all-to-all-start = ((bf16[32,8,1024]{2,1,0:T(8,128)(2,1)}), bf16[32,8,1024]{2,1,0:T(8,128)(2,1)S(1)}, u32[]{:S(2)}, u32[]{:S(2)}) async-start(bf16[32,8,1024]{2,1,0:T(8,128)(2,1)} %bitcast.2), calls=%async_computation | async-start | bytes 1048576 | tf_op jit(solution)/shard_map/all_to_all | solution.py:459
  12.5 16.0 %collective-permute-start.2 = (bf16[256,1024]{1,0:T(8,128)(2,1)}, bf16[256,1024]{1,0:T(8,128)(2,1)S(1)}, u32[]{:S(2)}, u32[]{:S(2)}) collective-permute-start(bf16[256,1024]{1,0:T(8,128)(2,1)} %refs_0_.2), channel_id=1, source_target_pairs={{0,1},{1,2},{2,3},{3,0},{4,5},{5,6},{6,7},{7,4},{8,9},{9,10},{10,1... | collective-permute-start | bytes 1572872 | tf_op jit(solution)/shard_map/ppermute | solution.py:38
  13.1 15.5 %collective-permute-start.3 = (bf16[256,1024]{1,0:T(8,128)(2,1)}, bf16[256,1024]{1,0:T(8,128)(2,1)S(1)}, u32[]{:S(2)}, u32[]{:S(2)}) collective-permute-start(bf16[256,1024]{1,0:T(8,128)(2,1)} %refs_0_.2), channel_id=1, source_target_pairs={{0,3},{1,0},{2,1},{3,2},{4,7},{5,4},{6,5},{7,6},{8,11},{9,8},{10,9... | collective-permute-start | bytes 1572872 | tf_op jit(solution)/shard_map/ppermute | solution.py:38
  14.6 8.4 %collective-permute-start.1 = (s32[1]{0:T(128)}, s32[1]{0:T(128)}, u32[]{:S(2)}, u32[]{:S(2)}) collective-permute-start(s32[1]{0:T(128)} %param.12), channel_id=1, source_target_pairs={{0,4},{4,0},{8,12},{12,8},{16,20},{20,16},{24,28},{28,24},{32,36},... | collective-permute-start | bytes 20 | tf_op jit(solution)/shard_map/ppermute | solution.py:34
  23.7 9.0 %all-to-all-start.1 = ((bf16[4,16,1024]{2,1,0:T(8,128)(2,1)}), bf16[4,16,1024]{2,1,0:T(8,128)(2,1)S(1)}, u32[]{:S(2)}, u32[]{:S(2)}) async-start(bf16[4,16,1024]{2,1,0:T(8,128)(2,1)} %broadcast_in_dim.2), calls=%async_computation.1 | async-start | bytes 262144 | tf_op jit(solution)/shard_map/all_to_all | solution.py:466
  28.6 18.5 %copy-start = (bf16[256,1024]{1,0:T(8,128)(2,1)}, bf16[256,1024]{1,0:T(8,128)(2,1)S(1)}, u32[]{:S(2)}) copy-start(bf16[256,1024]{1,0:T(8,128)(2,1)S(1)} %collective-permute-done.3.refs_4_) | copy-start | bytes 1572868
  28.6 15.6 %collective-permute-start.4 = (bf16[128,1024]{1,0:T(8,128)(2,1)S(1)}, bf16[128,1024]{1,0:T(8,128)(2,1)S(1)}, u32[]{:S(2)}, u32[]{:S(2)}) collective-permute-start(bf16[128,1024]{1,0:T(8,128)(2,1)S(1)} %slice.21), channel_id=1, source_target_pairs={{0,1},{1,2},{2,3},{3,0},{4,5},{5,6},{6,7},{7,4},{8,9},{9,10},{10,1... | collective-permute-start | bytes 786440 | tf_op jit(solution)/shard_map/ppermute | solution.py:38
  28.7 15.5 %collective-permute-start.5 = (bf16[128,1024]{1,0:T(8,128)(2,1)S(1)}, bf16[128,1024]{1,0:T(8,128)(2,1)S(1)}, u32[]{:S(2)}, u32[]{:S(2)}) collective-permute-start(bf16[128,1024]{1,0:T(8,128)(2,1)S(1)} %slice.22), channel_id=1, source_target_pairs={{0,3},{1,0},{2,1},{3,2},{4,7},{5,4},{6,5},{7,6},{8,11},{9,8},{10,9... | collective-permute-start | bytes 786440 | tf_op jit(solution)/shard_map/ppermute | solution.py:38
  38.6 13.6 %all-to-all-start.2 = ((bf16[16,8,1536]{2,1,0:T(8,128)(2,1)}), bf16[16,8,1536]{2,1,0:T(8,128)(2,1)S(1)}, u32[]{:S(2)}, u32[]{:S(2)}) async-start(bf16[16,8,1536]{2,1,0:T(8,128)(2,1)} %get-tuple-element.54), calls=%async_computation.2 | async-start | bytes 786432 | tf_op jit(solution)/shard_map/all_to_all | solution.py:30
  47.0 6.0 %collective-permute-start.6 = (bf16[272,512]{1,0:T(8,128)(2,1)S(1)}, bf16[272,512]{1,0:T(8,128)(2,1)S(1)}, u32[]{:S(2)}, u32[]{:S(2)}) collective-permute-start(bf16[272,512]{1,0:T(8,128)(2,1)S(1)} %shard_map.96.mine.kv), channel_id=1, source_target_pairs={{0,4},{4,0},{8,12},{12,8},{16,20},{20,16},{24,28},{28,24},{32,36},... | collective-permute-start | bytes 835592 | tf_op jit(solution)/shard_map/ppermute | solution.py:34
  51.5 11.8 %copy-start.1 = (bf16[256,1024]{1,0:T(8,128)(2,1)}, bf16[256,1024]{1,0:T(8,128)(2,1)S(1)}, u32[]{:S(2)}) copy-start(bf16[256,1024]{1,0:T(8,128)(2,1)S(1)} %shard_map.97.q_ref) | copy-start | bytes 1572868
  52.3 11.0 %collective-permute-start.7 = (bf16[128,512]{1,0:T(8,128)(2,1)S(1)}, bf16[128,512]{1,0:T(8,128)(2,1)S(1)}, u32[]{:S(2)}, u32[]{:S(2)}) collective-permute-start(bf16[128,512]{1,0:T(8,128)(2,1)S(1)} %slice.19), channel_id=1, source_target_pairs={{0,4},{4,0},{8,12},{12,8},{16,20},{20,16},{24,28},{28,24},{32,36},... | collective-permute-start | bytes 393224 | tf_op jit(solution)/shard_map/ppermute | solution.py:34
  56.3 15.9 %all-to-all-start.3 = ((bf16[16,8,1152]{2,1,0:T(8,128)(2,1)}), bf16[16,8,1152]{2,1,0:T(8,128)(2,1)S(1)}, u32[]{:S(2)}, u32[]{:S(2)}) async-start(bf16[16,8,1152]{2,1,0:T(8,128)(2,1)} %bitcast.6), calls=%async_computation.3 | async-start | bytes 589824 | tf_op jit(solution)/shard_map/all_to_all | solution.py:30
  72.2 9.5 %copy-start.4 = (bf16[256,1024]{1,0:T(8,128)(2,1)S(1)}, bf16[256,1024]{1,0:T(8,128)(2,1)}, u32[]{:S(2)}) copy-start(bf16[256,1024]{1,0:T(8,128)(2,1)} %get-tuple-element.70) | copy-start | bytes 1572868
  72.3 34.2 %copy-start.3 = (f32[256,1024]{1,0:T(8,128)S(1)}, f32[256,1024]{1,0:T(8,128)}, u32[]{:S(2)}) copy-start(f32[256,1024]{1,0:T(8,128)} %get-tuple-element.65) | copy-start | bytes 3145732
  76.4 5.4 %collective-permute-start.10 = (f32[8,1024]{1,0:T(8,128)S(1)}, f32[8,1024]{1,0:T(8,128)S(1)}, u32[]{:S(2)}, u32[]{:S(2)}) collective-permute-start(f32[8,1024]{1,0:T(8,128)S(1)} %get-tuple-element.72), channel_id=1, source_target_pairs={{0,1},{1,2},{2,3},{3,0},{4,5},{5,6},{6,7},{7,4},{8,9},{9,10},{10,1... | collective-permute-start | bytes 98312 | tf_op jit(solution)/shard_map/ppermute | solution.py:38
  78.2 5.5 %collective-permute-start.11 = (f32[8,1024]{1,0:T(8,128)S(1)}, f32[8,1024]{1,0:T(8,128)S(1)}, u32[]{:S(2)}, u32[]{:S(2)}) collective-permute-start(f32[8,1024]{1,0:T(8,128)S(1)} %get-tuple-element.73), channel_id=1, source_target_pairs={{0,2},{1,3},{2,0},{3,1},{4,6},{5,7},{6,4},{7,5},{8,10},{9,11},{10,... | collective-permute-start | bytes 98312 | tf_op jit(solution)/shard_map/ppermute | solution.py:38
  78.5 5.4 %collective-permute-start.12 = (f32[8,1024]{1,0:T(8,128)S(1)}, f32[8,1024]{1,0:T(8,128)S(1)}, u32[]{:S(2)}, u32[]{:S(2)}) collective-permute-start(f32[8,1024]{1,0:T(8,128)S(1)} %get-tuple-element.74), channel_id=1, source_target_pairs={{0,3},{1,0},{2,1},{3,2},{4,7},{5,4},{6,5},{7,6},{8,11},{9,8},{10,9... | collective-permute-start | bytes 98312 | tf_op jit(solution)/shard_map/ppermute | solution.py:38
  79.5 24.2 %collective-permute-start.8 = (bf16[256,1024]{1,0:T(8,128)(2,1)S(1)}, bf16[256,1024]{1,0:T(8,128)(2,1)S(1)}, u32[]{:S(2)}, u32[]{:S(2)}) collective-permute-start(bf16[256,1024]{1,0:T(8,128)(2,1)S(1)} %get-tuple-element.66), channel_id=1, source_target_pairs={{0,1},{1,2},{2,3},{3,0},{4,5},{5,6},{6,7},{7,4},{8,9},{9,10},{10,1... | collective-permute-start | bytes 1572872 | tf_op jit(solution)/shard_map/ppermute | solution.py:38
  81.8 22.0 %collective-permute-start.9 = (bf16[256,1024]{1,0:T(8,128)(2,1)S(1)}, bf16[256,1024]{1,0:T(8,128)(2,1)S(1)}, u32[]{:S(2)}, u32[]{:S(2)}) collective-permute-start(bf16[256,1024]{1,0:T(8,128)(2,1)S(1)} %copy-done.4), channel_id=1, source_target_pairs={{0,3},{1,0},{2,1},{3,2},{4,7},{5,4},{6,5},{7,6},{8,11},{9,8},{10,9... | collective-permute-start | bytes 1572872 | tf_op jit(solution)/shard_map/ppermute | solution.py:38
  84.0 22.4 %collective-permute-start.13 = (bf16[256,1024]{1,0:T(8,128)(2,1)S(1)}, bf16[256,1024]{1,0:T(8,128)(2,1)S(1)}, u32[]{:S(2)}, u32[]{:S(2)}) collective-permute-start(bf16[256,1024]{1,0:T(8,128)(2,1)S(1)} %get-tuple-element.75), channel_id=1, source_target_pairs={{0,2},{1,3},{2,0},{3,1},{4,6},{5,7},{6,4},{7,5},{8,10},{9,11},{10,... | collective-permute-start | bytes 1572872 | tf_op jit(solution)/shard_map/ppermute | solution.py:38

commit v2 on v1

--- a/solution.py
+++ b/solution.py
@@ -438,6 +438,34 @@
         out[pl.ds(at, total.shape[0]), :] = total
 
 
+def finish_kernel(own, a, b, c, query, block_out, query_out, staged, sems):
+    query_copy = pltpu.make_async_copy(query, query_out, sems.at[0])
+    query_copy.start()
+    total = own[...] + a[...].astype(jnp.float32)
+    total = total + b[...].astype(jnp.float32) + c[...].astype(jnp.float32)
+    staged[...] = total.astype(staged.dtype)
+    block_copy = pltpu.make_async_copy(staged, block_out, sems.at[1])
+    block_copy.start()
+    query_copy.wait()
+    block_copy.wait()
+
+
+def finish(*refs):
+    query = refs[-1]
+    return pl.pallas_call(
+        finish_kernel,
+        in_specs=[VMEM] * 5,
+        out_specs=[ANY] * 2,
+        out_shape=[jax.ShapeDtypeStruct(query.shape, query.dtype)] * 2,
+        scratch_shapes=[
+            pltpu.VMEM(query.shape, query.dtype),
+            pltpu.SemaphoreType.DMA((2,)),
+        ],
+        compiler_params=params(24),
+        cost_estimate=cost(1000, 4 * MIB),
+    )(*refs)
+
+
 def local(tokens, queries, valid_counts, query_host, w_query, w_key, w_value, w_out):
     host = query_host[0]
     blk, width = tokens.shape
@@ -491,10 +519,7 @@
     far, copies = lax.optimization_barrier((far, copies))
     far = head_shift(far, 2)
     query_out = lax.all_to_all(copies, "seq", 0, 0, tiled=True)
-    block_sum = own
-    for part in (*near, far):
-        block_sum += part.astype(jnp.float32)
-    return (block_sum.astype(dtype), query_out)
+    return tuple(finish(own, *near, far, query_out))
 
 
 def solution(mesh):

time: 109 us -> 109 us (level)
  blocking collectives: 17.7 us -> 0 us
  waiting for transfers between devices: 16.1 us -> 25.8 us
  starting transfers between devices: 37.8 us -> 45.1 us
  Pallas kernels: 32 us -> 33.9 us
  other arithmetic: 1.12 us -> 0.01 us
    all_to_all x1 -> x0, blocking collectives: 17.7 us -> none  [local(): query_out = lax.all_to_all(copies, 'seq', 0, 0, tiled=True)]
    ppermute x10, waiting for transfers between devices: 4.93 us -> 13.3 us  [head_shift(): return lax.ppermute(block, 'head', [(i, (i + step) % 4) for i in range(4)])]
    all_to_all x0 -> x1, starting transfers between devices: none -> 7.37 us  [local(): query_out = lax.all_to_all(copies, 'seq', 0, 0, tiled=True)]
    all_to_all x0 -> x1, waiting for transfers between devices: none -> 1.36 us  [local(): query_out = lax.all_to_all(copies, 'seq', 0, 0, tiled=True)]
    convert_element_type x1 -> x0, other arithmetic: 1.11 us -> none  [local(): return (block_sum.astype(dtype), query_out)]
  transfers between devices with their start and end apart: 17 -> 18, of which waited for: 6 -> 8; matrix products, arithmetic and copies ran while one was open for 1% -> 1% of each run, Pallas kernels for 23% -> 24%
where the time goes in v2:
time: 109 us; the launch traced here: 108 us
  starting transfers between devices  45.1 us (41%)
  Pallas kernels  33.9 us (31%)
  waiting for transfers between devices  25.8 us (24%)
  between operations  2.32 us (2%)
    ppermute x10, waiting for transfers between devices, head_shift(): return lax.ppermute(block, 'head', [(i, (i + step) % 4) for i in range(4)])  13.3 us
    all_to_all x2, starting transfers between devices, plane_swap(): lax.all_to_all(blocks, 'seq', 0, 0, axis_index_groups=PLANE, tiled=True)  12.5 us
    ppermute x10, starting transfers between devices, head_shift(): return lax.ppermute(block, 'head', [(i, (i + step) % 4) for i in range(4)])  11.6 us
    pallas_call x1, Pallas kernels, context(): pl.pallas_call(context_kernel, in_specs=[SMEM] + [VMEM] * 4 + [HBM], out_...  8.93 us
    all_to_all x1, starting transfers between devices, local(): spread = lax.all_to_all(sent, 'seq', 0, 0, tiled=True)  8.69 us
    all_to_all x1, waiting for transfers between devices, local(): spread = lax.all_to_all(sent, 'seq', 0, 0, tiled=True)  8.4 us
    all_to_all x1, starting transfers between devices, local(): query_out = lax.all_to_all(copies, 'seq', 0, 0, tiled=True)  7.37 us
    pallas_call x1, Pallas kernels, project_few(): pl.pallas_call(few_kernel, in_specs=[VMEM] + [HBM] * 3, out_specs=[VMEM]...  5.94 us
  transfers between devices with their start and end apart: 18, of which 8 were waited for; matrix products, arithmetic and copies ran while one was open for 1% of the time, Pallas kernels for 24%

profile of v2, /device:TPU:14, one launch (start us, length us, event | category | flops | bytes accessed | tf_op | source)
XLA Modules:
  0.0 107.9 jit_solution(12850421857947777116)
XLA Ops:
  1.3 2.5 %conditional.1 = (bf16[256,1024]{1,0:T(8,128)(2,1)}) conditional(s32[]{:T(128)} %bitcast, (s32[1]{0:T(128)}, bf16[256,1024]{1,0:T(8,128)(2,1)}, bf16[256,1024]{1,0:T(8,128)(2,1)}) %tuple.21, (bf16[256,1024]{1,0:T(8,128)(2,1)}, s32[1]{0:T(128)}, bf16[256,1024]{1,0:T(8,128)(2,1)}) %tuple.22), branch_computations={%region_0.0_spmd, %region_1.0_spmd} | conditional | flops 1000 | bytes 4194352 | solution.py:478
  1.3 2.5 %branch_0_fun.1 = bf16[256,1024]{1,0:T(8,128)(2,1)} custom-call(s32[1]{0:T(128)} %get-tuple-element.8.counts, bf16[256,1024]{1,0:T(8,128)(2,1)} %get-tuple-element.16.queries, bf16[256,1024]{1,0:T(8,128)(2,1)} %get-tuple-element.17.tokens), custom_call_target="tpu_custom_call" | custom-call | flops 1000 | bytes 2097152 | tf_op jit(solution)/shard_map/cond/branch_0_fun/pallas_call | solution.py:67
  3.8 8.7 %all-to-all-start = ((bf16[32,8,1024]{2,1,0:T(8,128)(2,1)}), bf16[32,8,1024]{2,1,0:T(8,128)(2,1)S(1)}, u32[]{:S(2)}, u32[]{:S(2)}) async-start(bf16[32,8,1024]{2,1,0:T(8,128)(2,1)} %bitcast.2), calls=%async_computation | async-start | bytes 1048576 | tf_op jit(solution)/shard_map/all_to_all | solution.py:487
  13.1 1.5 %collective-permute-start.3 = (bf16[256,1024]{1,0:T(8,128)(2,1)}, bf16[256,1024]{1,0:T(8,128)(2,1)S(1)}, u32[]{:S(2)}, u32[]{:S(2)}) collective-permute-start(bf16[256,1024]{1,0:T(8,128)(2,1)} %refs_0_.2), channel_id=1, source_target_pairs={{0,3},{1,0},{2,1},{3,2},{4,7},{5,4},{6,5},{7,6},{8,11},{9,8},{10,9... | collective-permute-start | bytes 1572872 | tf_op jit(solution)/shard_map/ppermute | solution.py:38
  14.6 8.4 %all-to-all-done = bf16[32,8,1024]{2,1,0:T(8,128)(2,1)S(1)} async-done(((bf16[32,8,1024]{2,1,0:T(8,128)(2,1)}), bf16[32,8,1024]{2,1,0:T(8,128)(2,1)S(1)}, u32[]{:S(2)}, u32[]{:S(2)}) %all-to-all-start) | async-done | bytes 524320 | tf_op jit(solution)/shard_map/all_to_all | solution.py:487
  23.7 4.8 %all-to-all-start.1 = ((bf16[4,16,1024]{2,1,0:T(8,128)(2,1)}), bf16[4,16,1024]{2,1,0:T(8,128)(2,1)S(1)}, u32[]{:S(2)}, u32[]{:S(2)}) async-start(bf16[4,16,1024]{2,1,0:T(8,128)(2,1)} %broadcast_in_dim.2), calls=%async_computation.1 | async-start | bytes 262144 | tf_op jit(solution)/shard_map/all_to_all | solution.py:494
  28.7 2.0 %collective-permute-start.5 = (bf16[128,1024]{1,0:T(8,128)(2,1)S(1)}, bf16[128,1024]{1,0:T(8,128)(2,1)S(1)}, u32[]{:S(2)}, u32[]{:S(2)}) collective-permute-start(bf16[128,1024]{1,0:T(8,128)(2,1)S(1)} %slice.22), channel_id=1, source_target_pairs={{0,3},{1,0},{2,1},{3,2},{4,7},{5,4},{6,5},{7,6},{8,11},{9,8},{10,9... | collective-permute-start | bytes 786440 | tf_op jit(solution)/shard_map/ppermute | solution.py:38
  30.7 2.0 %all-to-all-done.1.fews = bf16[4,16,1024]{2,1,0:T(8,128)(2,1)S(1)} async-done(((bf16[4,16,1024]{2,1,0:T(8,128)(2,1)}), bf16[4,16,1024]{2,1,0:T(8,128)(2,1)S(1)}, u32[]{:S(2)}, u32[]{:S(2)}) %all-to-all-start.1) | async-done | bytes 131104 | tf_op jit(solution)/shard_map/all_to_all | solution.py:494
  32.7 5.9 %shard_map.95 = (bf16[16,8,1536]{2,1,0:T(8,128)(2,1)}, bf16[16,512]{1,0:T(8,128)(2,1)S(1)}) custom-call(bf16[4,16,1024]{2,1,0:T(8,128)(2,1)S(1)} %all-to-all-done.1.fews, bf16[4096,1024]{1,0:T(8,128)(2,1)} %refs_5_.3, bf16[4096,256]{1,0:T(8,128)(2,1)} %refs_5_.2, bf16[4096,256]{1,0:T(8,128)(2,1)} %refs_6_.1), custom_call_target="tpu_custom_call" | custom-call | flops 1610612736 | bytes 12582912 | tf_op jit(solution)/shard_map/pallas_call | solution.py:123
  38.6 5.6 %all-to-all-start.2 = ((bf16[16,8,1536]{2,1,0:T(8,128)(2,1)}), bf16[16,8,1536]{2,1,0:T(8,128)(2,1)S(1)}, u32[]{:S(2)}, u32[]{:S(2)}) async-start(bf16[16,8,1536]{2,1,0:T(8,128)(2,1)} %get-tuple-element.54), calls=%async_computation.2 | async-start | bytes 786432 | tf_op jit(solution)/shard_map/all_to_all | solution.py:30
  44.2 2.8 %shard_map.96.mine.kv = bf16[272,512]{1,0:T(8,128)(2,1)S(1)} custom-call(bf16[256,1024]{1,0:T(8,128)(2,1)S(1)} %copy-done.3, bf16[256,1024]{1,0:T(8,128)(2,1)S(1)} %collective-permute-done.2.refs_1_, bf16[128,1024]{1,0:T(8,128)(2,1)S(1)} %collective-permute-done.4.refs_2_, bf16[128,1024]{1,0:T(8,128)(2,1)S(1)} %collective-permute-done.5.refs_3_, ...), custom_call_target="tpu_custom_call" | custom-call | flops 1073741824 | bytes 6291456 | tf_op jit(solution)/shard_map/pallas_call | solution.py:186
  47.1 4.3 %shard_map.97.q_ref = bf16[256,1024]{1,0:T(8,128)(2,1)S(1)} custom-call(bf16[256,1024]{1,0:T(8,128)(2,1)S(1)} %copy-done.3, bf16[256,1024]{1,0:T(8,128)(2,1)S(1)} %collective-permute-done.2.refs_1_, bf16[128,1024]{1,0:T(8,128)(2,1)S(1)} %collective-permute-done.4.refs_2_, bf16[128,1024]{1,0:T(8,128)(2,1)S(1)} %collective-permute-done.5.refs_3_, ...), custom_call_target="tpu_custom_call" | custom-call | flops 2147483648 | bytes 10485760 | tf_op jit(solution)/shard_map/pallas_call | solution.py:233
  53.0 3.4 %shard_map.98 = bf16[128,1152]{1,0:T(8,128)(2,1)} custom-call(s32[1]{0:T(128)S(6)} %copy.12.counts, s32[1]{0:T(128)} %collective-permute-done.1.sibling, bf16[128,1536]{1,0:T(8,128)(2,1)S(1)} %bitcast.11, bf16[272,512]{1,0:T(8,128)(2,1)S(1)} %shard_map.96.mine.kv, bf16[272,512]{1,0:T(8,128)(2,1)S(1)} %collective-permute-done.6.other), custom_call_target="tpu_custom_call" | custom-call | flops 335544320 | bytes 4194304 | tf_op jit(solution)/shard_map/pallas_call | solution.py:303
  56.4 7.0 %all-to-all-start.3 = ((bf16[16,8,1152]{2,1,0:T(8,128)(2,1)}), bf16[16,8,1152]{2,1,0:T(8,128)(2,1)S(1)}, u32[]{:S(2)}, u32[]{:S(2)}) async-start(bf16[16,8,1152]{2,1,0:T(8,128)(2,1)} %bitcast.6), calls=%async_computation.3 | async-start | bytes 589824 | tf_op jit(solution)/shard_map/all_to_all | solution.py:30
  63.4 8.9 %shard_map.99 = (bf16[256,1024]{1,0:T(8,128)(2,1)}, bf16[256,1024]{1,0:T(8,128)(2,1)}, bf16[256,1024]{1,0:T(8,128)(2,1)}, f32[256,1024]{1,0:T(8,128)}) custom-call(s32[1]{0:T(128)S(6)} %copy.12.counts, bf16[256,1024]{1,0:T(8,128)(2,1)} %copy-done.2, bf16[272,512]{1,0:T(8,128)(2,1)S(1)} %shard_map.96.mine.kv, bf16[128,1536]{1,0:T(8,128)(2,1)S(1)} %bitcast.12, ...), custom_call_target="tpu_custom_call" | custom-call | flops 2684354560 | bytes 12582912 | tf_op jit(solution)/shard_map/pallas_call | solution.py:376
  72.3 4.1 %shard_map.100 = (f32[8,1024]{1,0:T(8,128)S(1)}, f32[8,1024]{1,0:T(8,128)S(1)}, f32[8,1024]{1,0:T(8,128)S(1)}, f32[8,1024]{1,0:T(8,128)S(1)}) custom-call(bf16[16,8,1152]{2,1,0:T(8,128)(2,1)S(1)} %all-to-all-done.3.parts, bf16[1024,4096]{1,0:T(8,128)(2,1)} %w_ref.3), custom_call_target="tpu_custom_call" | custom-call | flops 1073741824 | bytes 8388608 | tf_op jit(solution)/shard_map/pallas_call | solution.py:420
  76.4 1.8 %collective-permute-start.10 = (f32[8,1024]{1,0:T(8,128)S(1)}, f32[8,1024]{1,0:T(8,128)S(1)}, u32[]{:S(2)}, u32[]{:S(2)}) collective-permute-start(f32[8,1024]{1,0:T(8,128)S(1)} %get-tuple-element.72), channel_id=1, source_target_pairs={{0,1},{1,2},{2,3},{3,0},{4,5},{5,6},{6,7},{7,4},{8,9},{9,10},{10,1... | collective-permute-start | bytes 98312 | tf_op jit(solution)/shard_map/ppermute | solution.py:38
  79.5 2.3 %collective-permute-start.8 = (bf16[256,1024]{1,0:T(8,128)(2,1)}, bf16[256,1024]{1,0:T(8,128)(2,1)S(1)}, u32[]{:S(2)}, u32[]{:S(2)}) collective-permute-start(bf16[256,1024]{1,0:T(8,128)(2,1)} %get-tuple-element.66), channel_id=1, source_target_pairs={{0,1},{1,2},{2,3},{3,0},{4,5},{5,6},{6,7},{7,4},{8,9},{9,10},{10,1... | collective-permute-start | bytes 1572872 | tf_op jit(solution)/shard_map/ppermute | solution.py:38
  81.8 1.9 %collective-permute-done.11.c = f32[8,1024]{1,0:T(8,128)S(1)} collective-permute-done((f32[8,1024]{1,0:T(8,128)S(1)}, f32[8,1024]{1,0:T(8,128)S(1)}, u32[]{:S(2)}, u32[]{:S(2)}) %collective-permute-start.11) | collective-permute-done | bytes 32800 | tf_op jit(solution)/shard_map/ppermute | solution.py:38
  84.9 2.0 %collective-permute-start.13 = (bf16[256,1024]{1,0:T(8,128)(2,1)}, bf16[256,1024]{1,0:T(8,128)(2,1)S(1)}, u32[]{:S(2)}, u32[]{:S(2)}) collective-permute-start(bf16[256,1024]{1,0:T(8,128)(2,1)} %get-tuple-element.75), channel_id=1, source_target_pairs={{0,2},{1,3},{2,0},{3,1},{4,6},{5,7},{6,4},{7,5},{8,10},{9,11},{10,... | collective-permute-start | bytes 1572872 | tf_op jit(solution)/shard_map/ppermute | solution.py:38
  86.9 7.4 %all-to-all-start.4 = ((bf16[32,8,1024]{2,1,0:T(8,128)(2,1)}), bf16[32,8,1024]{2,1,0:T(8,128)(2,1)S(1)}, u32[]{:S(2)}, u32[]{:S(2)}) async-start(bf16[32,8,1024]{2,1,0:T(8,128)(2,1)} %bitcast.7), calls=%async_computation.4 | async-start | bytes 1048576 | tf_op jit(solution)/shard_map/all_to_all | solution.py:521
  94.3 9.1 %collective-permute-done.8.a = bf16[256,1024]{1,0:T(8,128)(2,1)S(1)} collective-permute-done((bf16[256,1024]{1,0:T(8,128)(2,1)}, bf16[256,1024]{1,0:T(8,128)(2,1)S(1)}, u32[]{:S(2)}, u32[]{:S(2)}) %collective-permute-start.8) | collective-permute-done | bytes 524320 | tf_op jit(solution)/shard_map/ppermute | solution.py:38
  103.4 1.4 %all-to-all-done.4 = bf16[32,8,1024]{2,1,0:T(8,128)(2,1)S(1)} async-done(((bf16[32,8,1024]{2,1,0:T(8,128)(2,1)}), bf16[32,8,1024]{2,1,0:T(8,128)(2,1)S(1)}, u32[]{:S(2)}, u32[]{:S(2)}) %all-to-all-start.4) | async-done | bytes 524320 | tf_op jit(solution)/shard_map/all_to_all | solution.py:521
  104.8 1.9 %collective-permute-done.13.c = bf16[256,1024]{1,0:T(8,128)(2,1)S(1)} collective-permute-done((bf16[256,1024]{1,0:T(8,128)(2,1)}, bf16[256,1024]{1,0:T(8,128)(2,1)S(1)}, u32[]{:S(2)}, u32[]{:S(2)}) %collective-permute-start.13) | collective-permute-done | bytes 524320 | tf_op jit(solution)/shard_map/ppermute | solution.py:38
  (37 shorter events, 5.8 us)
Async XLA Ops:
  3.8 40.4 %copy-start.3 = (bf16[256,1024]{1,0:T(8,128)(2,1)S(1)}, bf16[256,1024]{1,0:T(8,128)(2,1)}, u32[]{:S(2)}) copy-start(bf16[256,1024]{1,0:T(8,128)(2,1)} %refs_0_.2) | copy-start | bytes 1572868
  3.8 19.2 %all-to-all-start = ((bf16[32,8,1024]{2,1,0:T(8,128)(2,1)}), bf16[32,8,1024]{2,1,0:T(8,128)(2,1)S(1)}, u32[]{:S(2)}, u32[]{:S(2)}) async-start(bf16[32,8,1024]{2,1,0:T(8,128)(2,1)} %bitcast.2), calls=%async_computation | async-start | bytes 1048576 | tf_op jit(solution)/shard_map/all_to_all | solution.py:487
  12.5 16.0 %collective-permute-start.2 = (bf16[256,1024]{1,0:T(8,128)(2,1)}, bf16[256,1024]{1,0:T(8,128)(2,1)S(1)}, u32[]{:S(2)}, u32[]{:S(2)}) collective-permute-start(bf16[256,1024]{1,0:T(8,128)(2,1)} %refs_0_.2), channel_id=1, source_target_pairs={{0,1},{1,2},{2,3},{3,0},{4,5},{5,6},{6,7},{7,4},{8,9},{9,10},{10,1... | collective-permute-start | bytes 1572872 | tf_op jit(solution)/shard_map/ppermute | solution.py:38
  13.1 15.5 %collective-permute-start.3 = (bf16[256,1024]{1,0:T(8,128)(2,1)}, bf16[256,1024]{1,0:T(8,128)(2,1)S(1)}, u32[]{:S(2)}, u32[]{:S(2)}) collective-permute-start(bf16[256,1024]{1,0:T(8,128)(2,1)} %refs_0_.2), channel_id=1, source_target_pairs={{0,3},{1,0},{2,1},{3,2},{4,7},{5,4},{6,5},{7,6},{8,11},{9,8},{10,9... | collective-permute-start | bytes 1572872 | tf_op jit(solution)/shard_map/ppermute | solution.py:38
  14.6 8.4 %collective-permute-start.1 = (s32[1]{0:T(128)}, s32[1]{0:T(128)}, u32[]{:S(2)}, u32[]{:S(2)}) collective-permute-start(s32[1]{0:T(128)} %param.12), channel_id=1, source_target_pairs={{0,4},{4,0},{8,12},{12,8},{16,20},{20,16},{24,28},{28,24},{32,36},... | collective-permute-start | bytes 20 | tf_op jit(solution)/shard_map/ppermute | solution.py:34
  23.7 9.0 %all-to-all-start.1 = ((bf16[4,16,1024]{2,1,0:T(8,128)(2,1)}), bf16[4,16,1024]{2,1,0:T(8,128)(2,1)S(1)}, u32[]{:S(2)}, u32[]{:S(2)}) async-start(bf16[4,16,1024]{2,1,0:T(8,128)(2,1)} %broadcast_in_dim.2), calls=%async_computation.1 | async-start | bytes 262144 | tf_op jit(solution)/shard_map/all_to_all | solution.py:494
  28.6 18.5 %copy-start = (bf16[256,1024]{1,0:T(8,128)(2,1)}, bf16[256,1024]{1,0:T(8,128)(2,1)S(1)}, u32[]{:S(2)}) copy-start(bf16[256,1024]{1,0:T(8,128)(2,1)S(1)} %collective-permute-done.3.refs_4_) | copy-start | bytes 1572868
  28.6 15.6 %collective-permute-start.4 = (bf16[128,1024]{1,0:T(8,128)(2,1)S(1)}, bf16[128,1024]{1,0:T(8,128)(2,1)S(1)}, u32[]{:S(2)}, u32[]{:S(2)}) collective-permute-start(bf16[128,1024]{1,0:T(8,128)(2,1)S(1)} %slice.21), channel_id=1, source_target_pairs={{0,1},{1,2},{2,3},{3,0},{4,5},{5,6},{6,7},{7,4},{8,9},{9,10},{10,1... | collective-permute-start | bytes 786440 | tf_op jit(solution)/shard_map/ppermute | solution.py:38
  28.7 15.5 %collective-permute-start.5 = (bf16[128,1024]{1,0:T(8,128)(2,1)S(1)}, bf16[128,1024]{1,0:T(8,128)(2,1)S(1)}, u32[]{:S(2)}, u32[]{:S(2)}) collective-permute-start(bf16[128,1024]{1,0:T(8,128)(2,1)S(1)} %slice.22), channel_id=1, source_target_pairs={{0,3},{1,0},{2,1},{3,2},{4,7},{5,4},{6,5},{7,6},{8,11},{9,8},{10,9... | collective-permute-start | bytes 786440 | tf_op jit(solution)/shard_map/ppermute | solution.py:38
  38.6 13.6 %all-to-all-start.2 = ((bf16[16,8,1536]{2,1,0:T(8,128)(2,1)}), bf16[16,8,1536]{2,1,0:T(8,128)(2,1)S(1)}, u32[]{:S(2)}, u32[]{:S(2)}) async-start(bf16[16,8,1536]{2,1,0:T(8,128)(2,1)} %get-tuple-element.54), calls=%async_computation.2 | async-start | bytes 786432 | tf_op jit(solution)/shard_map/all_to_all | solution.py:30
  47.0 6.0 %collective-permute-start.6 = (bf16[272,512]{1,0:T(8,128)(2,1)S(1)}, bf16[272,512]{1,0:T(8,128)(2,1)S(1)}, u32[]{:S(2)}, u32[]{:S(2)}) collective-permute-start(bf16[272,512]{1,0:T(8,128)(2,1)S(1)} %shard_map.96.mine.kv), channel_id=1, source_target_pairs={{0,4},{4,0},{8,12},{12,8},{16,20},{20,16},{24,28},{28,24},{32,36},... | collective-permute-start | bytes 835592 | tf_op jit(solution)/shard_map/ppermute | solution.py:34
  51.5 11.9 %copy-start.2 = (bf16[256,1024]{1,0:T(8,128)(2,1)}, bf16[256,1024]{1,0:T(8,128)(2,1)S(1)}, u32[]{:S(2)}) copy-start(bf16[256,1024]{1,0:T(8,128)(2,1)S(1)} %shard_map.97.q_ref) | copy-start | bytes 1572868
  52.3 11.1 %collective-permute-start.7 = (bf16[128,512]{1,0:T(8,128)(2,1)S(1)}, bf16[128,512]{1,0:T(8,128)(2,1)S(1)}, u32[]{:S(2)}, u32[]{:S(2)}) collective-permute-start(bf16[128,512]{1,0:T(8,128)(2,1)S(1)} %slice.19), channel_id=1, source_target_pairs={{0,4},{4,0},{8,12},{12,8},{16,20},{20,16},{24,28},{28,24},{32,36},... | collective-permute-start | bytes 393224 | tf_op jit(solution)/shard_map/ppermute | solution.py:34
  56.4 15.9 %all-to-all-start.3 = ((bf16[16,8,1152]{2,1,0:T(8,128)(2,1)}), bf16[16,8,1152]{2,1,0:T(8,128)(2,1)S(1)}, u32[]{:S(2)}, u32[]{:S(2)}) async-start(bf16[16,8,1152]{2,1,0:T(8,128)(2,1)} %bitcast.6), calls=%async_computation.3 | async-start | bytes 589824 | tf_op jit(solution)/shard_map/all_to_all | solution.py:30
  72.3 34.4 %copy-start.1 = (f32[256,1024]{1,0:T(8,128)S(1)}, f32[256,1024]{1,0:T(8,128)}, u32[]{:S(2)}) copy-start(f32[256,1024]{1,0:T(8,128)} %get-tuple-element.65.own) | copy-start | bytes 3145732
  76.4 5.4 %collective-permute-start.10 = (f32[8,1024]{1,0:T(8,128)S(1)}, f32[8,1024]{1,0:T(8,128)S(1)}, u32[]{:S(2)}, u32[]{:S(2)}) collective-permute-start(f32[8,1024]{1,0:T(8,128)S(1)} %get-tuple-element.72), channel_id=1, source_target_pairs={{0,1},{1,2},{2,3},{3,0},{4,5},{5,6},{6,7},{7,4},{8,9},{9,10},{10,1... | collective-permute-start | bytes 98312 | tf_op jit(solution)/shard_map/ppermute | solution.py:38
  78.2 5.5 %collective-permute-start.11 = (f32[8,1024]{1,0:T(8,128)S(1)}, f32[8,1024]{1,0:T(8,128)S(1)}, u32[]{:S(2)}, u32[]{:S(2)}) collective-permute-start(f32[8,1024]{1,0:T(8,128)S(1)} %get-tuple-element.73), channel_id=1, source_target_pairs={{0,2},{1,3},{2,0},{3,1},{4,6},{5,7},{6,4},{7,5},{8,10},{9,11},{10,... | collective-permute-start | bytes 98312 | tf_op jit(solution)/shard_map/ppermute | solution.py:38
  78.6 5.4 %collective-permute-start.12 = (f32[8,1024]{1,0:T(8,128)S(1)}, f32[8,1024]{1,0:T(8,128)S(1)}, u32[]{:S(2)}, u32[]{:S(2)}) collective-permute-start(f32[8,1024]{1,0:T(8,128)S(1)} %get-tuple-element.74), channel_id=1, source_target_pairs={{0,3},{1,0},{2,1},{3,2},{4,7},{5,4},{6,5},{7,6},{8,11},{9,8},{10,9... | collective-permute-start | bytes 98312 | tf_op jit(solution)/shard_map/ppermute | solution.py:38
  79.5 23.9 %collective-permute-start.8 = (bf16[256,1024]{1,0:T(8,128)(2,1)}, bf16[256,1024]{1,0:T(8,128)(2,1)S(1)}, u32[]{:S(2)}, u32[]{:S(2)}) collective-permute-start(bf16[256,1024]{1,0:T(8,128)(2,1)} %get-tuple-element.66), channel_id=1, source_target_pairs={{0,1},{1,2},{2,3},{3,0},{4,5},{5,6},{6,7},{7,4},{8,9},{9,10},{10,1... | collective-permute-start | bytes 1572872 | tf_op jit(solution)/shard_map/ppermute | solution.py:38
  81.8 21.6 %collective-permute-start.9 = (bf16[256,1024]{1,0:T(8,128)(2,1)}, bf16[256,1024]{1,0:T(8,128)(2,1)S(1)}, u32[]{:S(2)}, u32[]{:S(2)}) collective-permute-start(bf16[256,1024]{1,0:T(8,128)(2,1)} %get-tuple-element.70), channel_id=1, source_target_pairs={{0,3},{1,0},{2,1},{3,2},{4,7},{5,4},{6,5},{7,6},{8,11},{9,8},{10,9... | collective-permute-start | bytes 1572872 | tf_op jit(solution)/shard_map/ppermute | solution.py:38
  84.9 21.8 %collective-permute-start.13 = (bf16[256,1024]{1,0:T(8,128)(2,1)}, bf16[256,1024]{1,0:T(8,128)(2,1)S(1)}, u32[]{:S(2)}, u32[]{:S(2)}) collective-permute-start(bf16[256,1024]{1,0:T(8,128)(2,1)} %get-tuple-element.75), channel_id=1, source_target_pairs={{0,2},{1,3},{2,0},{3,1},{4,6},{5,7},{6,4},{7,5},{8,10},{9,11},{10,... | collective-permute-start | bytes 1572872 | tf_op jit(solution)/shard_map/ppermute | solution.py:38
  86.9 17.9 %all-to-all-start.4 = ((bf16[32,8,1024]{2,1,0:T(8,128)(2,1)}), bf16[32,8,1024]{2,1,0:T(8,128)(2,1)S(1)}, u32[]{:S(2)}, u32[]{:S(2)}) async-start(bf16[32,8,1024]{2,1,0:T(8,128)(2,1)} %bitcast.7), calls=%async_computation.4 | async-start | bytes 1048576 | tf_op jit(solution)/shard_map/all_to_all | solution.py:521
